TPU v7x, 32 devices: a whole 2x2x4 slice. The times are simulated.
32 devices in a mesh: cell: 8 (over y, x, core), spot: 4 (over z).
Axes of the slice: x: 2, y: 2, z: 4, core: 2. Of those that a mesh axis runs over, the one named last changes fastest.
Arguments:
- logits: float32 [11264, 8192], P('cell', 'spot'), may hold values from -10 to 10
- expression: float32 [11264, 2048], P('cell', 'spot'), may hold values from 0.05 to 20
- spatial: float32 [2048, 8192], P('cell', 'spot'), may hold values from 0.05 to 20
- cell_counts: int32 [11264], P('cell'), may hold values from 1 to 12
- spot_density: float32 [8192], P('spot'), may hold values from 0.5 to 8
- slide_id: int32 [8192], P('spot'), may hold values from 0 to 1
- padding: int32 [8192], P('spot'), may hold values 0 or 1
Outputs:
- losses: float32 [2], replicated
- grad_logits: float32 [11264, 8192], P('cell', 'spot')
- grad_expression: float32 [11264, 2048], P('cell', 'spot')
All inputs are finite; a program needn't handle non-finite values. No bound on the sum of `padding` on one device may be relied on, other than what follows from the above.
Results may differ from a plain program's by a relative error of at most 0.0003.
Values sent between devices are 32-bit elements; how exact they have to be, the bound alone decides.
A program may use at most 128 MiB of HBM per device.

v0:
```python
import jax
import jax.numpy as jnp
from jax import lax
from jax.sharding import PartitionSpec as P

epsilon = 1e-06
highest = lax.Precision.HIGHEST


def contract_cells(left, right):
    return lax.dot_general(
        left, right, (((0,), (0,)), ((), ())), precision=highest, preferred_element_type=jnp.float32
    )


def local(logits, expression, spatial, cell_counts, spot_density, slide_id, padding):
    weights = cell_counts.astype(jnp.float32)
    valid = (1 - padding).astype(jnp.float32)
    slide_masks = jnp.stack(
        [valid * (slide_id == 0).astype(jnp.float32), valid * (slide_id == 1).astype(jnp.float32)]
    )
    column_peak = lax.pmax(jnp.max(logits, axis=0), "cell")
    exponent = jnp.exp(logits - column_peak)
    column_total, weighted_total = lax.psum(
        (jnp.sum(exponent, axis=0), jnp.dot(weights, exponent, precision=highest)), "cell"
    )
    mapping = exponent / column_total
    density = weighted_total / column_total
    gathered = lax.all_gather(expression, "spot", axis=1, tiled=True)
    genes_all = gathered.shape[1]
    predicted = lax.psum_scatter(
        contract_cells(gathered, mapping), "cell", scatter_dimension=0, tiled=True
    )
    spot_dot, spot_aa, spot_bb = lax.psum(
        (
            jnp.sum(predicted * spatial, axis=0),
            jnp.sum(predicted * predicted, axis=0),
            jnp.sum(spatial * spatial, axis=0),
        ),
        "cell",
    )
    spot_norm = jnp.sqrt((spot_aa + epsilon) * (spot_bb + epsilon))
    spot_cos = spot_dot / spot_norm
    masks_t = slide_masks.T
    local_slide = jnp.stack(
        [
            spot_density,
            density,
            spot_density * jnp.log(spot_density),
            spot_density * jnp.log(density),
            jnp.ones_like(density),
            spot_cos,
        ],
        axis=1,
    )
    gene_dot, gene_aa, gene_bb, per_slide = lax.psum(
        (
            jnp.dot(predicted * spatial, masks_t, precision=highest),
            jnp.dot(predicted * predicted, masks_t, precision=highest),
            jnp.dot(spatial * spatial, masks_t, precision=highest),
            jnp.dot(slide_masks, local_slide, precision=highest),
        ),
        "spot",
    )
    gene_norm = jnp.sqrt((gene_aa + epsilon) * (gene_bb + epsilon))
    gene_cos = gene_dot / gene_norm
    gene_cos_sum = jnp.sum(gene_cos, axis=0)
    gene_cos_sum = lax.psum(gene_cos_sum, "cell")
    mass_target = per_slide[:, 0]
    mass_pred = per_slide[:, 1]
    live_spots = jnp.maximum(per_slide[:, 4], 1.0)
    divergence = (
        (per_slide[:, 2] - per_slide[:, 3]) / mass_target
        - jnp.log(mass_target)
        + jnp.log(mass_pred)
    )
    losses = -gene_cos_sum / genes_all - per_slide[:, 5] / live_spots + divergence
    inv_spread = jnp.dot(1.0 / gene_norm, slide_masks, precision=highest)
    corr_spread = jnp.dot(gene_cos / (gene_aa + epsilon), slide_masks, precision=highest)
    grad_pred = -(spatial * inv_spread - predicted * corr_spread) / genes_all
    spot_weight = jnp.dot(1.0 / live_spots, slide_masks, precision=highest)
    grad_pred = grad_pred - spot_weight * (
        spatial / spot_norm - spot_cos * predicted / (spot_aa + epsilon)
    )
    grad_density = (
        jnp.dot(1.0 / mass_pred, slide_masks, precision=highest)
        - spot_density * jnp.dot(1.0 / mass_target, slide_masks, precision=highest) / density
    )
    full_grad = lax.all_gather(grad_pred, "cell", axis=0, tiled=True)
    grad_map = (
        jnp.dot(gathered, full_grad, precision=highest, preferred_element_type=jnp.float32)
        + weights[:, None] * grad_density[None, :]
    )
    column_dot = lax.psum(jnp.sum(mapping * grad_map, axis=0), "cell")
    grad_logits = mapping * (grad_map - column_dot)
    partial_grad = lax.dot_general(
        mapping,
        full_grad,
        (((1,), (1,)), ((), ())),
        precision=highest,
        preferred_element_type=jnp.float32,
    )
    grad_expression = lax.psum_scatter(partial_grad, "spot", scatter_dimension=1, tiled=True)
    return (losses, grad_logits, grad_expression)


def solution(mesh):
    in_specs = (
        P("cell", "spot"),
        P("cell", "spot"),
        P("cell", "spot"),
        P("cell"),
        P("spot"),
        P("spot"),
        P("spot"),
    )
    out_specs = (P(), P("cell", "spot"), P("cell", "spot"))
    return jax.shard_map(local, mesh=mesh, in_specs=in_specs, out_specs=out_specs, check_vma=False)
```

profile of v0, /device:TPU:9, one launch (start us, length us, event | category | flops | bytes accessed | tf_op | source)
XLA Modules:
  0.0 853.1 jit_solution(17700742403843024281)
XLA Ops:
  7.2 0.7 all-gather.3.cloned.1.call-update
  7.9 4.9 reduce_max.9
  12.8 12.0 %pmax.7 = f32[2048]{0:T(1024)S(1)} all-reduce(f32[2048]{0:T(1024)S(1)} %reduce_max.9), channel_id=1, replica_groups=mesh['cell'=8,'spot'=4] {'cell'}, use_global_device_ids=true, to_apply=%region_1.0 | all-reduce | flops 2048 | bytes 16384 | tf_op jit(solution)/shard_map/pmax | solution.py:22
  24.9 6.5 fusion.2
  31.3 13.5 %psum.77 = f32[2048]{0:T(1024)S(1)} all-reduce(f32[2048]{0:T(1024)S(1)} %fusion.2), channel_id=1, replica_groups=mesh['cell'=8,'spot'=4] {'cell'}, use_global_device_ids=true, to_apply=%region_3.0 | all-reduce | flops 2048 | bytes 16384 | tf_op jit(solution)/shard_map/psum | solution.py:24
  44.8 164.2 %all-gather.3.cloned.1.call-done = f32[1408,2048]{1,0:T(8,128)} async-done(((f32[1408,512]{1,0:T(8,128)}), f32[1408,2048]{1,0:T(8,128)}) %all-gather.3.cloned.1.call-update) | async-done | bytes 11534352 | tf_op jit(solution)/shard_map/all_gather | solution.py:29
  209.0 101.0 %convolution_bitcast_fusion = f32[2048,2048]{0,1:T(8,128)} fusion(f32[1408,2048]{1,0:T(8,128)} %all-gather.3.cloned.1.call-done, f32[1408,2048]{1,0:T(8,128)} %param.7, f32[2048]{0:T(1024)S(1)} %psum.77, f32[2048]{0:T(1024)S(1)} %pmax.7), kind=kOutput, calls=%fused_computation.7 | convolution fusion | flops 70872727552 | bytes 39862272 | tf_op jit(solution)/shard_map/dot_general | solution.py:11
  310.2 0.6 copy-done.3
  310.8 0.9 copy-done.1
  311.7 1.8 copy.15
  313.7 1.7 fusion.8
  315.4 11.4 %fusion = f32[1,2048]{1,0:T(1,128)S(1)} fusion(f32[1408,1]{0,1:T(1,128)S(1)} %reshape.30, f32[1408,2048]{1,0:T(8,128)} %param.7, f32[2048]{0:T(1024)S(1)} %pmax.7), kind=kOutput, calls=%fused_computation.4 | convolution fusion | flops 37486592 | bytes 11556352 | tf_op jit(solution)/shard_map/dot_general | solution.py:25
  326.8 100.4 %reduce-scatter.3.cloned.1.call-done = f32[256,2048]{0,1:T(8,128)} async-done(((f32[2048,2048]{0,1:T(8,128)}), f32[256,2048]{0,1:T(8,128)}) %reduce-scatter.3.cloned.1.call-update) | async-done | bytes 2097168 | tf_op jit(solution)/shard_map/reduce_scatter | solution.py:31
  427.2 3.0 multiply_reduce_fusion.2
  430.2 20.6 %all-reduce.1 = (f32[2048]{0:T(1024)S(1)}, f32[2048]{0:T(1024)S(1)}, f32[2048]{0:T(1024)S(1)}, f32[2048]{0:T(1024)S(1)}) all-reduce(f32[2048]{0:T(1024)S(1)} %bitcast.56, f32[2048]{0:T(1024)S(1)} %get-tuple-element.4, f32[2048]{0:T(1024)S(1)} %multiply_reduce_fusion.1, ...), channel_id=1, replica_groups=mesh['cell'=8,'spot'=4] {'cell'}, use_global_device_ids=true, to_apply=%region_10.0 | all-reduce | flops 8192 | bytes 65536 | tf_op jit(solution)/shard_map/psum | solution.py:24
  450.9 2.7 fusion.10
  453.6 3.4 fusion.12
  457.0 0.2 fusion.29
  457.2 7.2 all-reduce.2
  464.4 0.3 divide_reduce_fusion.1
  464.7 0.2 fusion.25
  464.9 2.0 convolution_multiply_fusion
  466.8 6.0 fusion.7
  472.9 98.2 %all-gather.5.cloned.1.call-done = f32[2048,2048]{0,1:T(8,128)} async-done(((f32[256,2048]{0,1:T(8,128)}), f32[2048,2048]{0,1:T(8,128)}) %all-gather.5.cloned.1.call-update) | async-done | bytes 16777232 | tf_op jit(solution)/shard_map/all_gather | solution.py:89
  571.1 80.6 %fusion.30 = f32[1408,2048]{1,0:T(8,128)} fusion(f32[2048,2048]{0,1:T(8,128)} %all-gather.5.cloned.1.call-done, f32[1408,2048]{1,0:T(8,128)} %param.7, f32[2048]{0:T(1024)S(1)} %psum.77, f32[2048]{0:T(1024)S(1)} %pmax.7), kind=kOutput, calls=%fused_computation.57 | convolution fusion | flops 70872727552 | bytes 39862272 | tf_op jit(solution)/shard_map/dot_general | solution.py:96
  651.8 0.2 fusion.21
  652.0 0.2 fusion.23
  652.2 84.3 %multiply_reduce_fusion = (f32[2048]{0:T(1024)S(1)}, f32[2048,1408]{0,1:T(8,128)}) fusion(f32[2048]{0:T(1024)S(1)} %divide_subtract_fusion, f32[1408]{0:T(1024)S(1)} %convert_element_type.9, f32[2048]{0:T(1024)S(1)} %psum.77, f32[1408,2048]{1,0:T(8,128)} %param.7, f32[2048]{0:T(1024)S(1)} %pmax.7, f32[2048,2048]{0,1:T(8,128)} %all-gather.5.cloned.1.call-done, ...), kind=kOutput, calls=%fused_computation.2 | convolution fusion | flops 70884261888 | bytes 51418624 | tf_op jit(solution)/shard_map/dot_general | solution.py:91
  736.5 11.8 %all-reduce = (f32[2]{0:T(128)S(1)}, f32[2048]{0:T(1024)S(1)}) all-reduce(f32[2]{0:T(128)S(1)} %divide_reduce_fusion, f32[2048]{0:T(1024)S(1)} %get-tuple-element.28), channel_id=1, replica_groups=mesh['cell'=8,'spot'=4] {'cell'}, use_global_device_ids=true, to_apply=%region_9.0 | all-reduce | flops 2050 | bytes 16400 | tf_op jit(solution)/shard_map/psum | solution.py:68
  748.3 0.5 subtract_add_fusion
  748.8 14.4 %subtract_multiply_fusion = f32[1408,2048]{1,0:T(8,128)} fusion(f32[2048,1408]{0,1:T(8,128)} %get-tuple-element.29, f32[2048]{0:T(1024)S(1)} %get-tuple-element.11, f32[2048]{0:T(1024)S(1)} %divide_subtract_fusion, f32[1408]{0:T(1024)S(1)} %convert_element_type.9, f32[2048]{0:T(1024)S(1)} %psum.77, f32[1408,2048]{1,0:T(8,128)} %param.7, f32[2048]{0:T(1024)S(1)} %pmax.7), kind=kLoop, calls=%fused_computation.1 | loop fusion | flops 17301504 | bytes 34641408 | tf_op jit(solution)/shard_map/mul | solution.py:95
  763.2 83.2 %reduce-scatter.5.cloned.1.call-done = f32[1408,512]{1,0:T(8,128)} async-done(((f32[1408,2048]{1,0:T(8,128)}), f32[1408,512]{1,0:T(8,128)}) %reduce-scatter.5.cloned.1.call-update) | async-done | bytes 2883600 | tf_op jit(solution)/shard_map/reduce_scatter | solution.py:103
  (26 shorter events, 0.7 us)
Async XLA Ops:
  7.2 201.8 %all-gather.3.cloned.1.call-start = ((), (), s32[]{:S(2)}) async-start(), calls=%async_computation.2 | async-start | bytes 14417920 | tf_op jit(solution)/shard_map/all_gather | solution.py:29
  7.9 419.3 %reduce-scatter.3.cloned.1.call-start = ((), (), s32[]{:S(2)}) async-start(), calls=%async_computation.3 | async-start | bytes 18874368 | tf_op jit(solution)/shard_map/reduce_scatter | solution.py:31
  310.0 0.7 copy-start.3
  310.1 1.6 copy-start.1
  310.1 3.6 copy-start.4
  310.1 3.6 copy-start.5
  310.1 261.0 %all-gather.5.cloned.1.call-start = ((), (), s32[]{:S(2)}) async-start(), calls=%async_computation.4 | async-start | bytes 18874368 | tf_op jit(solution)/shard_map/all_gather | solution.py:89
  315.4 135.4 %copy-start.2 = (f32[2048]{0:T(1024)S(1)}, f32[2048]{0:T(1024)}, u32[]{:S(2)}) copy-start(f32[2048]{0:T(1024)} %param.11) | copy-start | bytes 24580
  427.2 37.6 %copy-start = (f32[256,2048]{0,1:T(8,128)S(1)}, f32[256,2048]{0,1:T(8,128)}, u32[]{:S(2)}) copy-start(f32[256,2048]{0,1:T(8,128)} %reduce-scatter.3.cloned.1.call-done) | copy-start | bytes 6291460
  472.9 373.5 %reduce-scatter.5.cloned.1.call-start = ((), (), s32[]{:S(2)}) async-start(), calls=%async_computation.5 | async-start | bytes 14417920 | tf_op jit(solution)/shard_map/reduce_scatter | solution.py:103
Sparse Core Ops, SparseCore 0:
  9.6 199.3 all-gather.2
  310.2 116.9 reduce-scatter.2
  473.0 98.0 all-gather.4
  651.8 194.5 reduce-scatter.4
where the time goes:
time: 858 us; the launch traced here: 853 us
  waiting for transfers between devices  447 us (52%)
  matrix products  294 us (34%)
  blocking collectives  65 us (8%)
  other arithmetic  29.8 us (3%)
  between operations  14.2 us (2%)
    all_gather x1, waiting for transfers between devices, local(): gathered = lax.all_gather(expression, 'spot', axis=1, tiled=True)  164 us
    dot_general x1, matrix products, contract_cells(): lax.dot_general(left, right, (((0,), (0,)), ((), ())), precision=highest,...  101 us
    reduce_scatter x1, waiting for transfers between devices, local(): lax.psum_scatter(contract_cells(gathered, mapping), 'cell', scatter_dimen...  100 us
    all_gather x1, waiting for transfers between devices, local(): full_grad = lax.all_gather(grad_pred, 'cell', axis=0, tiled=True)  98.2 us
    dot_general x1, matrix products, local(): jnp.dot(gathered, full_grad, precision=highest, preferred_element_type=jn...  84.3 us
    reduce_scatter x1, waiting for transfers between devices, local(): lax.psum_scatter(partial_grad, 'spot', scatter_dimension=1, tiled=True)  83.2 us
    dot_general x1, matrix products, local(): lax.dot_general(mapping, full_grad, (((1,), (1,)), ((), ())), precision=h...  80.6 us
    psum x2, blocking collectives, local(): lax.psum((jnp.sum(exponent, axis=0), jnp.dot(weights, exponent, precision...  34 us
  transfers between devices with their start and end apart: 4, of which 4 were waited for; matrix products, arithmetic and copies ran while one was open for 15% of the time, Pallas kernels for 0%

commit v1 on v0

v1 whole, which is shorter than its diff:
```python
import functools

import jax
import jax.numpy as jnp
from jax import lax
from jax.experimental import pallas as pl
from jax.experimental.pallas import tpu as pltpu
from jax.sharding import PartitionSpec as P

epsilon = 1e-06
MESH = pl.DeviceIdType.MESH
F32, BF16 = jnp.float32, jnp.bfloat16
TN = (((0,), (0,)), ((), ()))
NN = (((1,), (0,)), ((), ()))
NT = (((1,), (1,)), ((), ()))


def dot(left, right, dims=NN):
    return lax.dot_general(left, right, dims, preferred_element_type=F32)


def split(v):
    high = v.astype(BF16)
    return high, (v - high.astype(F32)).astype(BF16)


def arrival(z, i, planes, per):
    near = jnp.minimum(z, planes - 1 - z)
    j = jnp.maximum(i - per, 0)
    pair = lax.rem(j, 2 * per)
    t = 1 + lax.div(j, 2 * per)
    both = jnp.where(lax.rem(pair, 2) == 0, z - t, z + t)
    late = jnp.maximum(j - 2 * near * per, 0)
    t = near + 1 + lax.div(late, per)
    one = jnp.where(z < planes - 1 - z, z + t, z - t)
    in_pairs = j < 2 * near * per
    shard = jnp.where(i < per, z, jnp.where(in_pairs, both, one))
    chunk = jnp.where(i < per, i, jnp.where(in_pairs, lax.div(pair, 2), lax.rem(late, per)))
    return shard, chunk


def greet(c, z, cells, planes):
    barrier = pltpu.get_barrier_semaphore()

    def in_plane(step, _):
        pl.semaphore_signal(barrier, inc=1, device_id=(lax.rem(c + step, cells), z), device_id_type=MESH)
        return 0

    def in_column(step, _):
        pl.semaphore_signal(barrier, inc=1, device_id=(c, lax.rem(z + step, planes)), device_id_type=MESH)
        return 0

    lax.fori_loop(1, cells, in_plane, 0)
    lax.fori_loop(1, planes, in_column, 0)
    pl.semaphore_wait(barrier, cells + planes - 2)


def share(src, dst, send, recv, me, count, device):
    def start(step, _):
        other = lax.rem(me + step, count)
        pltpu.make_async_remote_copy(
            src_ref=src, dst_ref=dst.at[me], send_sem=send.at[other], recv_sem=recv.at[me],
            device_id=device(other), device_id_type=MESH,
        ).start()
        return 0

    lax.fori_loop(1, count, start, 0)


def collect(src, dst, send, recv, me, count, device):
    def wait(step, total):
        other = lax.rem(me + step, count)
        copy = pltpu.make_async_remote_copy(
            src_ref=src, dst_ref=dst.at[other], send_sem=send.at[other], recv_sem=recv.at[other],
            device_id=device(other), device_id_type=MESH,
        )
        copy.wait_send()
        copy.wait_recv()
        return total + dst[other]

    return lax.fori_loop(1, count, wait, src[...])


def forward_kernel(
    cfg, logits, expr, spatial, counts, dens, slide, pad,
    gath, ehi_out, elo_out, gp_out, vec_out, loss_out,
    ehi, elo, lbuf, stage, amat, partial, corer, half, chipr, pred, spat,
    tots, totr, acc, spots, spotr, gcol, gst, gstr, vec,
    g_recv, up_send, down_send, l_sem, st_sem, core_send, core_recv, chip_send, chip_recv,
    spat_send, spat_recv, tot_send, tot_recv, spot_send, spot_recv, gst_send, gst_recv, out_sem,
):
    cells, planes, C, S, G, GK, r = (cfg[k] for k in ("cells", "planes", "C", "S", "G", "GK", "r"))
    chips, per, chunks = cells // 2, G // planes // GK, G // GK
    rows, tile = cfg["rows"], cfg["tile"]
    own_genes = G // cells
    c, z = lax.axis_index("cell"), lax.axis_index("spot")
    chip, core = lax.div(c, 2), lax.rem(c, 2)
    sibling = c + 1 - 2 * core
    in_plane = lambda other: (other, z)
    in_column = lambda other: (c, other)

    greet(c, z, cells, planes)

    def z_copy(src, g, to, send):
        return pltpu.make_async_remote_copy(
            src_ref=src, dst_ref=gath.at[g], send_sem=send.at[g], recv_sem=g_recv.at[g],
            device_id=(c, to), device_id_type=MESH,
        )

    up, down = jnp.minimum(z + 1, planes - 1), jnp.maximum(z - 1, 0)

    def send_own(k, _):
        g = z * per + k
        src = expr.at[:, pl.ds(pl.multiple_of(k * GK, 128), GK)]

        @pl.when(z < planes - 1)
        def _():
            z_copy(src, g, up, up_send).start()

        @pl.when(z > 0)
        def _():
            z_copy(src, g, down, down_send).start()

        pltpu.make_async_copy(src, gath.at[g], g_recv.at[g]).start()
        return 0

    lax.fori_loop(0, per, send_own, 0)

    blocks = own_genes // r

    def spat_copy(b):
        place = c * blocks + b
        g, owner = lax.div(place, cells), lax.rem(place, cells)
        src = spatial.at[pl.ds(pl.multiple_of(b * r, 8), r)]
        remote = pltpu.make_async_remote_copy(
            src_ref=src, dst_ref=spat.at[g], send_sem=spat_send.at[b], recv_sem=spat_recv.at[g],
            device_id=(owner, z), device_id_type=MESH,
        )
        local = pltpu.make_async_copy(src, spat.at[g], spat_recv.at[g])
        return owner, remote, local

    def send_spat(b, _):
        owner, remote, local = spat_copy(b)

        @pl.when(owner != c)
        def _():
            remote.start()

        @pl.when(owner == c)
        def _():
            local.start()

        return 0

    lax.fori_loop(0, blocks, send_spat, 0)

    def load(t):
        return pltpu.make_async_copy(
            logits.at[pl.ds(pl.multiple_of(t * rows, rows), rows)], lbuf.at[lax.rem(t, 2)], l_sem.at[lax.rem(t, 2)]
        )

    load(0).start()

    def exps(t, _):
        @pl.when(t + 1 < C // rows)
        def _():
            load(t + 1).start()

        load(t).wait()
        high, low = split(jnp.exp(lbuf[lax.rem(t, 2)]))
        place = pl.ds(pl.multiple_of(t * rows, rows), rows)
        ehi[place, :] = high
        elo[place, :] = low
        return 0

    lax.fori_loop(0, C // rows, exps, 0)
    keep = [pltpu.make_async_copy(ehi, ehi_out, out_sem.at[0]), pltpu.make_async_copy(elo, elo_out, out_sem.at[1])]
    for copy in keep:
        copy.start()

    row = lax.broadcasted_iota(jnp.int32, (16, C), 0)
    weight = jnp.broadcast_to(counts[...].astype(F32), (16, C))
    lhs = jnp.where(row == 0, 1.0, jnp.where(row == 1, weight, 0.0)).astype(BF16)

    def sums(t, _):
        place = pl.ds(pl.multiple_of(t * tile, tile), tile)
        both = dot(lhs, ehi[:, place]) + dot(lhs, elo[:, place])
        tots[:, place] = both[:8]
        return 0

    lax.fori_loop(0, S // tile, sums, 0)
    share(tots, totr, tot_send, tot_recv, c, cells, in_plane)

    valid = (1 - pad[...]).astype(F32)
    mask0 = valid * (slide[...] == 0).astype(F32)
    mask1 = valid * (slide[...] == 1).astype(F32)
    vec[4:5, :] = mask0
    vec[5:6, :] = mask1
    acc[...] = jnp.zeros_like(acc)
    gcol[...] = jnp.zeros_like(gcol)

    def core_copy(g, slot):
        return pltpu.make_async_remote_copy(
            src_ref=partial.at[slot, :, 1 - core], dst_ref=corer.at[g], send_sem=core_send.at[slot],
            recv_sem=core_recv.at[g], device_id=(sibling, z), device_id_type=MESH,
        )

    def chip_copy(g, slot, other):
        return pltpu.make_async_remote_copy(
            src_ref=half.at[slot, other], dst_ref=chipr.at[g, chip], send_sem=chip_send.at[slot, other],
            recv_sem=chip_recv.at[g, chip], device_id=(2 * other + core, z), device_id_type=MESH,
        )

    def chip_wait(g, slot, other):
        return pltpu.make_async_remote_copy(
            src_ref=half.at[slot, chip], dst_ref=chipr.at[g, other], send_sem=chip_send.at[slot, other],
            recv_sem=chip_recv.at[g, other], device_id=(2 * other + core, z), device_id_type=MESH,
        )

    def product(i):
        d, k = arrival(z, i, planes, per)
        g, slot = d * per + k, lax.rem(i, 2)
        z_copy(gath.at[g], g, down, down_send).wait_recv()

        @pl.when((d < z) & (z < planes - 1))
        def _():
            z_copy(gath.at[g], g, up, up_send).start()

        @pl.when((d > z) & (z > 0))
        def _():
            z_copy(gath.at[g], g, down, down_send).start()

        pull = pltpu.make_async_copy(gath.at[g], stage, st_sem)
        pull.start()
        pull.wait()

        @pl.when(i >= 2)
        def _():
            core_copy(g, slot).wait_send()

        def turn(t, _):
            place = pl.ds(pl.multiple_of(t * 128, 128), 128)
            high, low = split(stage[place, :].T)
            amat[:GK, place] = high
            amat[GK:, place] = low
            return 0

        lax.fori_loop(0, C // 128, turn, 0)

        def multiply(t, _):
            place = pl.ds(pl.multiple_of(t * tile, tile), tile)
            both = dot(amat[...], ehi[:, place])
            total = both[:GK] + both[GK:] + dot(amat[:GK, :], elo[:, place])
            partial[slot, :, :, :, place] = total.reshape(chips, 2, r, tile)
            return 0

        lax.fori_loop(0, S // tile, multiply, 0)
        core_copy(g, slot).start()

    def to_chips(i):
        d, k = arrival(z, i, planes, per)
        g, slot = d * per + k, lax.rem(i, 2)
        core_copy(g, slot).wait_recv()

        @pl.when(i >= 2)
        def _():
            def drain(step, _):
                chip_copy(g, slot, lax.rem(chip + step, chips)).wait_send()
                return 0

            lax.fori_loop(1, chips, drain, 0)

        def add(other, _):
            half[slot, other] = partial[slot, other, core] + corer[g, other]

            @pl.when(other != chip)
            def _():
                chip_copy(g, slot, other).start()

            return 0

        lax.fori_loop(0, chips, add, 0)

    def finish(i):
        d, k = arrival(z, i, planes, per)
        g, slot = d * per + k, lax.rem(i, 2)
        pltpu.make_async_copy(spat.at[g], spat.at[g], spat_recv.at[g]).wait()

        def add(step, total):
            other = lax.rem(chip + step, chips)
            chip_wait(g, slot, other).wait_recv()
            return total + chipr[g, other]

        p = lax.fori_loop(1, chips, add, half[slot, chip]) * vec[0:1, :]
        s = spat[g]
        pred[g] = p
        ps, pp, ss = p * s, p * p, s * s
        acc[0] += ps
        acc[1] += pp
        acc[2] += ss
        lane = lax.broadcasted_iota(jnp.int32, (r, 128), 1)
        cols = jnp.zeros((r, 128), F32)
        for n, v in enumerate((ps, pp, ss)):
            for m in range(2):
                one = jnp.sum(v * vec[4 + m : 5 + m, :], axis=1, keepdims=True)
                cols = jnp.where(lane == 2 * n + m, one, cols)
        gcol[pl.ds(pl.multiple_of(g * r, 8), r), :] = cols

    def step(i, _):
        @pl.when(i < chunks)
        def _():
            product(i)

        @pl.when(i == 1)
        def _():
            total = collect(tots, totr, tot_send, tot_recv, c, cells, in_plane)
            vec[0:1, :] = 1.0 / total[0:1, :]
            vec[1:2, :] = total[1:2, :] / total[0:1, :]

        @pl.when((i >= 1) & (i <= chunks))
        def _():
            to_chips(i - 1)

        @pl.when(i >= 2)
        def _():
            finish(i - 2)

        return 0

    lax.fori_loop(0, chunks + 2, step, 0)

    spots[...] = jnp.zeros_like(spots)
    for n in range(3):
        spots[n : n + 1, :] = jnp.sum(acc[n], axis=0, keepdims=True)
    share(spots, spotr, spot_send, spot_recv, c, cells, in_plane)
    gst[...] = jnp.zeros_like(gst)
    gst[0:8, :] = gcol[...].T[0:8, :]
    density = vec[1:2, :]
    target = dens[...]
    lane = lax.broadcasted_iota(jnp.int32, (1, gst.shape[1]), 1)
    logs = target * jnp.log(target), target * jnp.log(density)
    for n, v in enumerate((jnp.ones_like(target), target, density, *logs)):
        line = jnp.zeros((1, gst.shape[1]), F32)
        for m in range(2):
            one = jnp.sum(v * vec[4 + m : 5 + m, :], axis=1, keepdims=True)
            line = jnp.where(lane == m, one, line)
        gst[8 + n : 9 + n, :] = line
    share(gst, gstr, gst_send, gst_recv, z, planes, in_column)

    genes = collect(gst, gstr, gst_send, gst_recv, z, planes, in_column)
    dot_g, aa_g, bb_g = ([genes[2 * n + m : 2 * n + m + 1, :] for m in range(2)] for n in range(3))
    slides = [[genes[8 + n : 9 + n, m : m + 1] for m in range(2)] for n in range(5)]
    lines, cos_sums, own_losses = [], [], []
    for m in range(2):
        norm = jnp.sqrt((aa_g[m] + epsilon) * (bb_g[m] + epsilon))
        cos = dot_g[m] / norm
        lines += [-1.0 / (norm * G), cos / ((aa_g[m] + epsilon) * G)]
        cos_sums.append(jnp.sum(cos, axis=1, keepdims=True))
    lines.append(jnp.zeros((124, gst.shape[1]), F32))
    gcol[...] = jnp.concatenate(lines, axis=0).T
    live = [jnp.maximum(v, 1.0) for v in slides[0]]
    mass_target, mass_pred = slides[1], slides[2]
    divergence = [
        (slides[3][m] - slides[4][m]) / mass_target[m] - jnp.log(mass_target[m]) + jnp.log(mass_pred[m])
        for m in range(2)
    ]
    mask0, mask1 = vec[4:5, :], vec[5:6, :]
    grad_density = (
        mask0 / mass_pred[0] + mask1 / mass_pred[1]
        - dens[...] * (mask0 / mass_target[0] + mask1 / mass_target[1]) / vec[1:2, :]
    )
    spot_weight = mask0 / live[0] + mask1 / live[1]

    spot = collect(spots, spotr, spot_send, spot_recv, c, cells, in_plane)
    norm = jnp.sqrt((spot[1:2, :] + epsilon) * (spot[2:3, :] + epsilon))
    spot_cos = spot[0:1, :] / norm
    inverse = vec[0:1, :]
    vec[2:3, :] = -spot_weight / norm
    vec[3:4, :] = spot_weight * spot_cos / (spot[1:2, :] + epsilon)
    vec[6:7, :] = grad_density * inverse
    vec[7:8, :] = vec[1:2, :] * grad_density * inverse
    acc[0] = jnp.zeros((r, S), F32)

    def gradient(g, _):
        columns = gcol[pl.ds(pl.multiple_of(g * r, 8), r), :]
        by_spatial = vec[4:5, :] * columns[:, 0:1] + vec[5:6, :] * columns[:, 2:3] + vec[2:3, :]
        by_pred = vec[4:5, :] * columns[:, 1:2] + vec[5:6, :] * columns[:, 3:4] + vec[3:4, :]
        p = pred[g]
        value = (spat[g] * by_spatial + p * by_pred) * vec[0:1, :]
        acc[0] += p * value
        pred[g] = value
        return 0

    lax.fori_loop(0, chunks, gradient, 0)
    copy = pltpu.make_async_copy(pred, gp_out, out_sem.at[2])
    copy.start()
    vec_out[...] = jnp.zeros_like(vec_out)
    vec_out[0:1, :] = jnp.sum(acc[0], axis=0, keepdims=True)
    vec_out[8:9, :] = vec[6:7, :]
    vec_out[9:10, :] = vec[7:8, :]
    lane = lax.broadcasted_iota(jnp.int32, (1, 128), 1)
    spot_sums = [jnp.sum(vec[4 + m : 5 + m, :] * spot_cos, axis=1, keepdims=True) for m in range(2)]
    loss_out[...] = jnp.zeros_like(loss_out)
    for n, v in enumerate((cos_sums, spot_sums, live, divergence)):
        loss_out[n : n + 1, :] = jnp.where(lane == 0, v[0], jnp.where(lane == 1, v[1], 0.0))

    copy.wait()
    for copy in keep:
        copy.wait()

    def drain_z(g, _):
        d = lax.div(g, per)

        @pl.when((d <= z) & (z < planes - 1))
        def _():
            z_copy(gath.at[g], g, up, up_send).wait_send()

        @pl.when((d >= z) & (z > 0))
        def _():
            z_copy(gath.at[g], g, down, down_send).wait_send()

        return 0

    lax.fori_loop(0, chunks, drain_z, 0)

    def drain_spat(b, _):
        owner, remote, _ = spat_copy(b)

        @pl.when(owner != c)
        def _():
            remote.wait_send()

        return 0

    lax.fori_loop(0, blocks, drain_spat, 0)
    for slot in range(2):
        core_copy(0, slot).wait_send()

        def drain(step, _):
            chip_copy(0, slot, lax.rem(chip + step, chips)).wait_send()
            return 0

        lax.fori_loop(1, chips, drain, 0)


ANY = pl.BlockSpec(memory_space=pl.ANY)
VMEM = pl.BlockSpec(memory_space=pltpu.VMEM)


def forward(cfg, logits, expression, spatial, counts, dens, slide, pad):
    cells, planes, C, S, G, GK, r = (cfg[k] for k in ("cells", "planes", "C", "S", "G", "GK", "r"))
    chips, per, chunks = cells // 2, G // planes // GK, G // GK
    rows = cfg["rows"]
    wide = max(G // cells, 128)
    blocks = G // cells // r
    sem = pltpu.SemaphoreType.DMA
    scratch = [
        pltpu.VMEM((C, S), BF16), pltpu.VMEM((C, S), BF16), pltpu.VMEM((2, rows, S), F32),
        pltpu.VMEM((C, GK), F32), pltpu.VMEM((2 * GK, C), BF16),
        pltpu.VMEM((2, chips, 2, r, S), F32), pltpu.VMEM((chunks, chips, r, S), F32),
        pltpu.VMEM((2, chips, r, S), F32), pltpu.VMEM((chunks, chips, r, S), F32),
        pltpu.VMEM((chunks, r, S), F32), pltpu.VMEM((chunks, r, S), F32),
        pltpu.VMEM((8, S), F32), pltpu.VMEM((cells, 8, S), F32), pltpu.VMEM((3, r, S), F32),
        pltpu.VMEM((8, S), F32), pltpu.VMEM((cells, 8, S), F32), pltpu.VMEM((wide, 128), F32),
        pltpu.VMEM((16, wide), F32), pltpu.VMEM((planes, 16, wide), F32), pltpu.VMEM((8, S), F32),
        sem((chunks,)), sem((chunks,)), sem((chunks,)), sem((2,)), sem,
        sem((2,)), sem((chunks,)), sem((2, chips)), sem((chunks, chips)),
        sem((blocks,)), sem((chunks,)), sem((cells,)), sem((cells,)), sem((cells,)), sem((cells,)),
        sem((planes,)), sem((planes,)), sem((3,)),
    ]
    flops = 6 * C * S * G
    return pl.pallas_call(
        functools.partial(forward_kernel, cfg),
        out_shape=(
            jax.ShapeDtypeStruct((chunks, C, GK), F32),
            jax.ShapeDtypeStruct((C, S), BF16),
            jax.ShapeDtypeStruct((C, S), BF16),
            jax.ShapeDtypeStruct((chunks, r, S), F32),
            jax.ShapeDtypeStruct((16, S), F32),
            jax.ShapeDtypeStruct((8, 128), F32),
        ),
        in_specs=[ANY, ANY, ANY, VMEM, VMEM, VMEM, VMEM],
        out_specs=(ANY, ANY, ANY, ANY, VMEM, VMEM),
        scratch_shapes=scratch,
        compiler_params=pltpu.CompilerParams(
            collective_id=0, has_side_effects=True, vmem_limit_bytes=56 * 2**20
        ),
        cost_estimate=pl.CostEstimate(flops=flops, bytes_accessed=8 * C * S, transcendentals=C * S),
        name="forward",
    )(logits, expression, spatial, counts, dens, slide, pad)


def local(cells, planes, logits, expression, spatial, cell_counts, spot_density, slide_id, padding):
    C, S = logits.shape
    G = expression.shape[1] * planes
    GK = max(128, 8 * cells)
    cfg = dict(cells=cells, planes=planes, C=C, S=S, G=G, GK=GK, r=GK // cells, rows=128, tile=512)
    gath, ehi, elo, gp, vec, loss = forward(
        cfg, logits, expression, spatial, cell_counts[None, :], spot_density[None, :],
        slide_id[None, :], padding[None, :],
    )
    high = lax.Precision.HIGH
    full = lax.all_gather(gp, "cell", axis=1).reshape(G, S)
    gathered = gath.transpose(1, 0, 2).reshape(C, G)
    exponent = ehi.astype(F32) + elo.astype(F32)
    column = lax.psum(vec[0], "cell") + vec[9]
    cos_sum = lax.psum(loss[0, :2], "cell")
    spot_sum = lax.psum(loss[1, :2], "spot")
    losses = -cos_sum / G - spot_sum / loss[2, :2] + loss[3, :2]
    grad_map = jnp.dot(gathered, full, precision=high) + cell_counts.astype(F32)[:, None] * vec[8][None, :]
    grad_logits = exponent * (grad_map - column)
    partial_grad = lax.dot_general(exponent, full, NT, precision=high, preferred_element_type=F32)
    grad_expression = lax.psum_scatter(partial_grad, "spot", scatter_dimension=1, tiled=True)
    return (losses, grad_logits, grad_expression)


def solution(mesh):
    cells, planes = mesh.shape["cell"], mesh.shape["spot"]
    in_specs = (
        P("cell", "spot"), P("cell", "spot"), P("cell", "spot"), P("cell"), P("spot"), P("spot"), P("spot"),
    )
    out_specs = (P(), P("cell", "spot"), P("cell", "spot"))
    return jax.shard_map(
        functools.partial(local, cells, planes), mesh=mesh, in_specs=in_specs, out_specs=out_specs, check_vma=False
    )
```

time: 858 us -> 607 us (0.71)
  Pallas kernels: 0 us -> 256 us
  waiting for transfers between devices: 447 us -> 206 us
  matrix products: 294 us -> 91.2 us
  blocking collectives: 65 us -> 22 us
  other arithmetic: 29.8 us -> 0.53 us
  local copies, waits for them, and re-layouts: 3.41 us -> 14.8 us
    pallas_call x0 -> x1, Pallas kernels: none -> 256 us  [forward(): pl.pallas_call(functools.partial(forward_kernel, cfg), out_shape=(jax.Sha...]
    dot_general x13 -> x2, matrix products: 294 us -> 91.2 us  [the longest x1 47.9 us: local(): jnp.dot(gathered, full, precision=high)]
    all_gather x2 -> x1, waiting for transfers between devices: 262 us -> 94.9 us  [local(): full = lax.all_gather(gp, 'cell', axis=1).reshape(G, S)]
    reduce_scatter x1 -> x0, waiting for transfers between devices: 100 us -> none  [local(): lax.psum_scatter(contract_cells(gathered, mapping), 'cell', scatter_dimen...]
    psum x4 -> x2, blocking collectives: 53 us -> 22 us  [the longest x1 11.8 us: local(): cos_sum = lax.psum(loss[0, :2], 'cell')]
    reduce_scatter x1, waiting for transfers between devices: 83.2 us -> 111 us  [local(): lax.psum_scatter(partial_grad, 'spot', scatter_dimension=1, tiled=True)]
    mul x3 -> x0, other arithmetic: 14.4 us -> none  [the longest x1 14.4 us: local(): grad_logits = mapping * (grad_map - column_dot)]
    pmax x1 -> x0, blocking collectives: 12 us -> none  [local(): column_peak = lax.pmax(jnp.max(logits, axis=0), 'cell')]
  transfers between devices with their start and end apart: 4 -> 2, of which waited for: 4 -> 2; matrix products, arithmetic and copies ran while one was open for 15% -> 10% of each run, Pallas kernels for 0% -> 0%
where the time goes in v1:
time: 607 us; the launch traced here: 604 us
  Pallas kernels  256 us (42%)
  waiting for transfers between devices  206 us (34%)
  matrix products  91.2 us (15%)
  blocking collectives  22 us (4%)
  local copies, waits for them, and re-layouts  14.8 us (2%)
  between operations  14.1 us (2%)
    pallas_call x1, Pallas kernels, forward(): pl.pallas_call(functools.partial(forward_kernel, cfg), out_shape=(jax.Sha...  256 us
    reduce_scatter x1, waiting for transfers between devices, local(): lax.psum_scatter(partial_grad, 'spot', scatter_dimension=1, tiled=True)  111 us
    all_gather x1, waiting for transfers between devices, local(): full = lax.all_gather(gp, 'cell', axis=1).reshape(G, S)  94.9 us
    dot_general x1, matrix products, local(): jnp.dot(gathered, full, precision=high)  47.9 us
    dot_general x1, matrix products, local(): lax.dot_general(exponent, full, NT, precision=high, preferred_element_typ...  43.3 us
  transfers between devices with their start and end apart: 2, of which 2 were waited for; matrix products, arithmetic and copies ran while one was open for 10% of the time, Pallas kernels for 0%

profile of v1, /device:TPU:9, one launch (start us, length us, event | category | flops | bytes accessed | tf_op | source)
XLA Modules:
  0.0 604.4 jit_solution(10761642815659716293)
XLA Ops:
  7.2 0.0 all-gather.3.cloned.1.call-start
  7.2 1.3 broadcast_in_dim.14.counts
  8.5 255.5 %forward.1 = (f32[16,1408,128]{2,1,0:T(8,128)}, bf16[1408,2048]{1,0:T(8,128)(2,1)}, bf16[1408,2048]{1,0:T(8,128)(2,1)}, f32[16,16,2048]{2,1,0:T(8,128)}, f32[16,2048]{1,0:T(8,128)}, /*index=5*/f32[8,128]{1,0:T(8,128)}) custom-call(f32[1408,2048]{1,0:T(8,128)} %logits.1, f32[1408,512]{1,0:T(8,128)} %expr.1, f32[256,2048]{1,0:T(8,128)} %spatial.1, ...), custom_call_target="tpu_custom_call" | custom-call | flops 35433480192 | bytes 23068672 | tf_op jit(solution)/shard_map/forward/pallas_call | solution.py:472
  264.0 0.0 all-gather.3.cloned.1.call-update
  264.1 0.2 reduce-scatter.2.cloned.1.call-start
  264.3 94.9 %all-gather.3.cloned.1.call-done = f32[16,128,2048]{2,1,0:T(8,128)} async-done(((f32[16,16,2048]{2,1,0:T(8,128)}), f32[16,128,2048]{2,1,0:T(8,128)}) %all-gather.3.cloned.1.call-update) | async-done | bytes 16777232 | tf_op jit(solution)/shard_map/all_gather | solution.py:503
  359.2 43.3 %fusion = f32[1408,2048]{1,0:T(8,128)} fusion(f32[2048,2048]{1,0:T(8,128)} %bitcast.29, bf16[1408,2048]{1,0:T(8,128)(2,1)} %get-tuple-element.11, bf16[1408,2048]{1,0:T(8,128)(2,1)} %get-tuple-element.10), kind=kOutput, calls=%fused_computation.2 | convolution fusion | flops 35442130944 | bytes 39845888 | tf_op jit(solution)/shard_map/dot_general | solution.py:512
  402.5 0.0 copy-start.1
  402.5 0.0 copy-start
  402.5 0.0 reduce-scatter.2.cloned.1.call-update
  402.6 0.7 copy-done.1
  403.2 0.9 fusion.2
  404.1 11.8 %all-reduce = (f32[2]{0:T(128)S(1)}, f32[2048]{0:T(1024)S(1)}) all-reduce(f32[2]{0:T(128)S(1)} %get-tuple-element.20, f32[2048]{0:T(1024)S(1)} %bitcast.27), channel_id=1, replica_groups=mesh['cell'=8,'spot'=4] {'cell'}, use_global_device_ids=true, to_apply=%region_0.0 | all-reduce | flops 2050 | bytes 16400 | tf_op jit(solution)/shard_map/psum | solution.py:507
  416.0 10.1 %psum.22 = f32[2]{0:T(128)S(1)} all-reduce(f32[2]{0:T(128)S(1)} %get-tuple-element.21), channel_id=1, replica_groups=mesh['cell'=8,'spot'=4] {'spot'}, use_global_device_ids=true, to_apply=%region_1.0 | all-reduce | flops 2 | bytes 16 | tf_op jit(solution)/shard_map/psum | solution.py:508
  426.1 0.0 copy-done
  426.1 12.0 %copy.10 = f32[1408,16,128]{0,2,1:T(8,128)} copy(f32[1408,16,128]{2,0,1:T(8,128)} %bitcast.24) | data formatting | bytes 23068672 | tf_op jit(solution)/shard_map/transpose | solution.py:504
  438.1 0.5 bitcast_add_fusion
  438.6 47.9 %subtract_multiply_fusion = f32[1408,2048]{1,0:T(8,128)} fusion(bf16[1408,2048]{1,0:T(8,128)(2,1)} %get-tuple-element.11, bf16[1408,2048]{1,0:T(8,128)(2,1)} %get-tuple-element.10, f32[1408,2048]{0,1:T(8,128)} %bitcast.25, f32[2048,2048]{1,0:T(8,128)} %bitcast.30, f32[2048]{0:T(1024)S(1)} %add.23, f32[2048]{0:T(1024)S(1)} %bitcast.28, ...), kind=kOutput, calls=%fused_computation | convolution fusion | flops 35453665280 | bytes 51402240 | tf_op jit(solution)/shard_map/dot_general | solution.py:510
  486.5 111.0 %reduce-scatter.2.cloned.1.call-done = f32[1408,512]{1,0:T(8,128)} async-done(((f32[1408,2048]{1,0:T(8,128)}), f32[1408,512]{1,0:T(8,128)}) %reduce-scatter.2.cloned.1.call-update) | async-done | bytes 2883600 | tf_op jit(solution)/shard_map/reduce_scatter | solution.py:513
  (3 shorter events, 0.0 us)
Async XLA Ops:
  7.2 352.0 %all-gather.3.cloned.1.call-start = ((), (), s32[]{:S(2)}) async-start(), calls=%async_computation.2 | async-start | bytes 18874368 | tf_op jit(solution)/shard_map/all_gather | solution.py:503
  264.1 333.5 %reduce-scatter.2.cloned.1.call-start = ((), (), s32[]{:S(2)}) async-start(), calls=%async_computation.1 | async-start | bytes 14417920 | tf_op jit(solution)/shard_map/reduce_scatter | solution.py:513
  402.5 0.7 copy-start.1
  402.5 23.6 %copy-start = (s32[1408]{0:T(1024)S(1)}, s32[1408]{0:T(1024)}, u32[]{:S(2)}) copy-start(s32[1408]{0:T(1024)} %param.10) | copy-start | bytes 16900
Sparse Core Ops, SparseCore 0:
  264.2 94.9 all-gather.2
  402.7 194.8 reduce-scatter.1

commit v2 on v1

--- a/solution.py
+++ b/solution.py
@@ -399,9 +399,10 @@
     vec_out[8:9, :] = vec[6:7, :]
     vec_out[9:10, :] = vec[7:8, :]
     lane = lax.broadcasted_iota(jnp.int32, (1, 128), 1)
+    vec_out[1:2, 0:128] = jnp.where(lane == 0, cos_sums[0], jnp.where(lane == 1, cos_sums[1], 0.0))
     spot_sums = [jnp.sum(vec[4 + m : 5 + m, :] * spot_cos, axis=1, keepdims=True) for m in range(2)]
     loss_out[...] = jnp.zeros_like(loss_out)
-    for n, v in enumerate((cos_sums, spot_sums, live, divergence)):
+    for n, v in enumerate((spot_sums, live, divergence)):
         loss_out[n : n + 1, :] = jnp.where(lane == 0, v[0], jnp.where(lane == 1, v[1], 0.0))
 
     copy.wait()
@@ -490,28 +491,322 @@
     )(logits, expression, spatial, counts, dens, slide, pad)
 
 
+def backward_kernel(
+    cfg, gp, gath, ehi, elo, vec, loss, weight,
+    grad_logits, grad_expr, losses, gpland, below, above,
+    e2, x2, gph, gpl, gstage, xstage, zst, zsend, outst, cols, vecr, lossr,
+    e_sem, own_sem, gp_recv, own_send, fwd_send, gs_sem, xs_sem, b_recv, a_recv, zs_sem, zst_sem, out_sem,
+    vec_send, vec_recv, loss_send, loss_recv,
+):
+    cells, planes, C, S, G, GK, r = (cfg[k] for k in ("cells", "planes", "C", "S", "G", "GK", "r"))
+    chips, per, chunks = cells // 2, G // planes // GK, G // GK
+    parts, tile, slots = cfg["parts"], cfg["tile"], cfg["slots"]
+    rows, tiles = C // parts, S // tile
+    c, z = lax.axis_index("cell"), lax.axis_index("spot")
+    chip, core = lax.div(c, 2), lax.rem(c, 2)
+    sibling = c + 1 - 2 * core
+    in_plane = lambda other: (other, z)
+    in_column = lambda other: (c, other)
+    at_end = (z == 0) | (z == planes - 1)
+
+    def order(i):
+        d, k = arrival(z, chunks - 1 - i, planes, per)
+        return d, k, d * per + k
+
+    def e_copy(t, _=None):
+        place = pl.ds(pl.multiple_of(t * rows, 16), rows)
+        return (
+            pltpu.make_async_copy(ehi.at[place], e2.at[t, pl.ds(0, rows)], e_sem.at[0, t]),
+            pltpu.make_async_copy(elo.at[place], e2.at[t, pl.ds(rows, rows)], e_sem.at[1, t]),
+        )
+
+    greet(c, z, cells, planes)
+
+    def own_copy(g, other):
+        to = jnp.where(other == chip, sibling, 2 * other + core)
+        return pltpu.make_async_remote_copy(
+            src_ref=gp.at[g], dst_ref=gpland.at[g, c], send_sem=own_send.at[g, other], recv_sem=gp_recv.at[g, c],
+            device_id=(to, z), device_id_type=MESH,
+        )
+
+    def forward_copy(g, other):
+        source = 2 * other + core
+        return pltpu.make_async_remote_copy(
+            src_ref=gpland.at[g, source], dst_ref=gpland.at[g, source], send_sem=fwd_send.at[g, other],
+            recv_sem=gp_recv.at[g, source], device_id=(sibling, z), device_id_type=MESH,
+        )
+
+    def landed(g, source):
+        pltpu.make_async_copy(gpland.at[g, source], gpland.at[g, source], gp_recv.at[g, source]).wait()
+
+    def send_own(i):
+        _, _, g = order(i)
+
+        def start(step, _):
+            own_copy(g, lax.rem(chip + step, chips)).start()
+            return 0
+
+        lax.fori_loop(1, chips + 1, start, 0)
+        pltpu.make_async_copy(gp.at[g], gpland.at[g, c], own_sem.at[g]).start()
+
+    send_own(0)
+    send_own(1)
+    for t in range(parts):
+        for copy in e_copy(t):
+            copy.start()
+    mine = vec.at[pl.ds(0, 8)]
+    share(mine, vecr, vec_send, vec_recv, c, cells, in_plane)
+    share(loss, lossr, loss_send, loss_recv, z, planes, in_column)
+    for t in range(parts):
+        for copy in e_copy(t):
+            copy.wait()
+
+    def gather(i):
+        _, _, g = order(i)
+
+        @pl.when(i + 2 < chunks)
+        def _():
+            send_own(i + 2)
+
+        x_copy = pltpu.make_async_copy(gath.at[g], xstage, xs_sem)
+        x_copy.start()
+
+        def pass_on(step, _):
+            other = lax.rem(chip + step, chips)
+            landed(g, 2 * other + core)
+            forward_copy(g, other).start()
+            return 0
+
+        lax.fori_loop(1, chips, pass_on, 0)
+
+        def take(other, _):
+            landed(g, 2 * other + 1 - core)
+            return 0
+
+        lax.fori_loop(0, chips, take, 0)
+        pltpu.make_async_copy(gp.at[g], gpland.at[g, c], own_sem.at[g]).wait()
+        g_copy = pltpu.make_async_copy(gpland.at[g], gstage, gs_sem)
+        g_copy.start()
+        x_copy.wait()
+        columns = pl.ds(pl.multiple_of(g * GK, 128), GK)
+
+        def split_x(t, _):
+            high, low = split(xstage[pl.ds(pl.multiple_of(t * rows, 16), rows), :])
+            x2[t, pl.ds(0, rows), columns] = high
+            x2[t, pl.ds(rows, rows), columns] = low
+            return 0
+
+        lax.fori_loop(0, parts, split_x, 0)
+        g_copy.wait()
+
+        def split_g(t, _):
+            place = pl.ds(pl.multiple_of(t * 128, 128), 128)
+            high, low = split(gstage[:, :, place].reshape(GK, 128))
+            lines = pl.ds(pl.multiple_of(g * GK, 128), GK)
+            gph[lines, place] = high
+            gpl[lines, place] = low
+            return 0
+
+        lax.fori_loop(0, S // 128, split_g, 0)
+
+    def up_copy(g, slot):
+        return pltpu.make_async_remote_copy(
+            src_ref=zsend.at[slot], dst_ref=below.at[g], send_sem=zs_sem.at[slot], recv_sem=b_recv.at[g],
+            device_id=(c, jnp.minimum(z + 1, planes - 1)), device_id_type=MESH,
+        )
+
+    def down_copy(g, slot):
+        return pltpu.make_async_remote_copy(
+            src_ref=zsend.at[slot], dst_ref=above.at[g], send_sem=zs_sem.at[slot], recv_sem=a_recv.at[g],
+            device_id=(c, jnp.maximum(z - 1, 0)), device_id_type=MESH,
+        )
+
+    def sent(slot):
+        pltpu.make_async_copy(zsend.at[slot], zsend.at[slot], zs_sem.at[slot]).wait()
+
+    def expression_part(i):
+        d, k, g = order(i)
+        slot = lax.rem(i, 3)
+
+        @pl.when(i >= 3)
+        def _():
+            sent(slot)
+
+        lines = pl.ds(pl.multiple_of(g * GK, 128), GK)
+
+        def multiply(t, _):
+            both = dot(e2[t], gph[lines, :], NT)
+            total = both[:rows] + both[rows:] + dot(e2[t, pl.ds(0, rows)], gpl[lines, :], NT)
+            zsend[slot, pl.ds(pl.multiple_of(t * rows, 16), rows), :] = total
+            return 0
+
+        lax.fori_loop(0, parts, multiply, 0)
+
+        def take(source, recv):
+            pltpu.make_async_copy(source.at[g], source.at[g], recv.at[g]).wait()
+            copy = pltpu.make_async_copy(source.at[g], zst, zst_sem)
+            copy.start()
+            copy.wait()
+
+            def add(t, _):
+                place = pl.ds(pl.multiple_of(t * rows, 16), rows)
+                zsend[slot, place, :] += zst[place, :]
+                return 0
+
+            lax.fori_loop(0, parts, add, 0)
+
+        @pl.when((d >= z) & (z > 0))
+        def _():
+            take(below, b_recv)
+
+        @pl.when((d <= z) & (z < planes - 1))
+        def _():
+            take(above, a_recv)
+
+        @pl.when(d > z)
+        def _():
+            up_copy(g, slot).start()
+
+        @pl.when(d < z)
+        def _():
+            down_copy(g, slot).start()
+
+        @pl.when(d == z)
+        def _():
+            place = pl.ds(pl.multiple_of(k * GK, 128), GK)
+            pltpu.make_async_copy(zsend.at[slot], grad_expr.at[:, place], zs_sem.at[slot]).start()
+
+    def out_copy(j, slot):
+        t, n = lax.div(j, tiles), lax.rem(j, tiles)
+        return pltpu.make_async_copy(
+            outst.at[slot],
+            grad_logits.at[pl.ds(pl.multiple_of(t * rows, 8), rows), pl.ds(pl.multiple_of(n * tile, 128), tile)],
+            out_sem.at[slot],
+        )
+
+    def logits_part(j):
+        t, n = lax.div(j, tiles), lax.rem(j, tiles)
+        slot = lax.rem(j, 2)
+        place = pl.ds(pl.multiple_of(n * tile, 128), tile)
+
+        @pl.when(j >= 2)
+        def _():
+            out_copy(j - 2, slot).wait()
+
+        both = dot(x2[t], gph[:, place])
+        total = both[:rows] + both[rows:] + dot(x2[t, pl.ds(0, rows)], gpl[:, place])
+        scale = weight[pl.ds(pl.multiple_of(t * rows, 8), rows), :]
+        total = total + (scale * cols[0:1, place] - cols[1:2, place])
+        exponent = e2[t, pl.ds(0, rows), place].astype(F32) + e2[t, pl.ds(rows, rows), place].astype(F32)
+        outst[slot] = exponent * total
+        out_copy(j, slot).start()
+
+    def step(t, _):
+        @pl.when(t < chunks)
+        def _():
+            gather(t)
+
+        @pl.when(t == chunks)
+        def _():
+            total = collect(mine, vecr, vec_send, vec_recv, c, cells, in_plane)
+            spot_sum = collect(loss, lossr, loss_send, loss_recv, z, planes, in_column)
+            cols[0:1, :] = vec[8:9, :]
+            cols[1:2, :] = total[0:1, :] + vec[9:10, :]
+            losses[...] = jnp.zeros_like(losses)
+            losses[0:1, :] = loss[2:3, :] - total[1:2, 0:128] / G - spot_sum[0:1, :] / loss[1:2, :]
+
+        late = t - jnp.where(at_end, 0, cfg["late"])
+        i = lax.div(3 * jnp.maximum(late, 0) + 7, 8)
+
+        @pl.when((late >= 0) & (lax.div(8 * i, 3) == late) & (i < chunks))
+        def _():
+            expression_part(i)
+
+        @pl.when((t >= chunks) & (t < chunks + parts * tiles))
+        def _():
+            logits_part(t - chunks)
+
+        return 0
+
+    lax.fori_loop(0, slots, step, 0)
+
+    for slot in range(3):
+        sent(slot)
+    for j in range(parts * tiles - 2, parts * tiles):
+        out_copy(j, j % 2).wait()
+
+    def drain(g, _):
+        def one(step, _):
+            other = lax.rem(chip + step, chips)
+            own_copy(g, other).wait_send()
+
+            @pl.when(step < chips)
+            def _():
+                forward_copy(g, other).wait_send()
+
+            return 0
+
+        lax.fori_loop(1, chips + 1, one, 0)
+        return 0
+
+    lax.fori_loop(0, chunks, drain, 0)
+
+
+def backward(cfg, gp, gath, ehi, elo, vec, loss, weight):
+    cells, planes, C, S, G, GK, r = (cfg[k] for k in ("cells", "planes", "C", "S", "G", "GK", "r"))
+    chips, per, chunks = cells // 2, G // planes // GK, G // GK
+    parts, tile = cfg["parts"], cfg["tile"]
+    rows = C // parts
+    sem = pltpu.SemaphoreType.DMA
+    scratch = [
+        pltpu.VMEM((parts, 2 * rows, S), BF16), pltpu.VMEM((parts, 2 * rows, G), BF16),
+        pltpu.VMEM((G, S), BF16), pltpu.VMEM((G, S), BF16),
+        pltpu.VMEM((cells, r, S), F32), pltpu.VMEM((C, GK), F32), pltpu.VMEM((C, GK), F32),
+        pltpu.VMEM((3, C, GK), F32), pltpu.VMEM((2, rows, tile), F32),
+        pltpu.VMEM((8, S), F32), pltpu.VMEM((cells, 8, S), F32), pltpu.VMEM((planes, 8, 128), F32),
+        sem((2, parts)), sem((chunks,)), sem((chunks, cells)), sem((chunks, chips)), sem((chunks, chips)),
+        sem, sem, sem((chunks,)), sem((chunks,)), sem((3,)), sem, sem((2,)),
+        sem((cells,)), sem((cells,)), sem((planes,)), sem((planes,)),
+    ]
+    return pl.pallas_call(
+        functools.partial(backward_kernel, cfg),
+        out_shape=(
+            jax.ShapeDtypeStruct((C, S), F32),
+            jax.ShapeDtypeStruct((C, G // planes), F32),
+            jax.ShapeDtypeStruct((8, 128), F32),
+            jax.ShapeDtypeStruct((chunks, cells, r, S), F32),
+            jax.ShapeDtypeStruct((chunks, C, GK), F32),
+            jax.ShapeDtypeStruct((chunks, C, GK), F32),
+        ),
+        in_specs=[ANY, ANY, ANY, ANY, VMEM, VMEM, VMEM],
+        out_specs=(ANY, ANY, VMEM, ANY, ANY, ANY),
+        scratch_shapes=scratch,
+        compiler_params=pltpu.CompilerParams(
+            collective_id=1, has_side_effects=True, vmem_limit_bytes=60 * 2**20
+        ),
+        cost_estimate=pl.CostEstimate(flops=12 * C * S * G, bytes_accessed=16 * C * S, transcendentals=0),
+        name="backward",
+    )(gp, gath, ehi, elo, vec, loss, weight)
+
+
 def local(cells, planes, logits, expression, spatial, cell_counts, spot_density, slide_id, padding):
     C, S = logits.shape
     G = expression.shape[1] * planes
     GK = max(128, 8 * cells)
-    cfg = dict(cells=cells, planes=planes, C=C, S=S, G=G, GK=GK, r=GK // cells, rows=128, tile=512)
+    chunks, parts, tile, late = G // GK, 4, 512, 5
+    slots = max(chunks + parts * (S // tile), late + 8 * (chunks - 1) // 3 + 1)
+    cfg = dict(
+        cells=cells, planes=planes, C=C, S=S, G=G, GK=GK, r=GK // cells, rows=128, tile=tile, parts=parts,
+        late=late, slots=slots,
+    )
     gath, ehi, elo, gp, vec, loss = forward(
         cfg, logits, expression, spatial, cell_counts[None, :], spot_density[None, :],
         slide_id[None, :], padding[None, :],
     )
-    high = lax.Precision.HIGH
-    full = lax.all_gather(gp, "cell", axis=1).reshape(G, S)
-    gathered = gath.transpose(1, 0, 2).reshape(C, G)
-    exponent = ehi.astype(F32) + elo.astype(F32)
-    column = lax.psum(vec[0], "cell") + vec[9]
-    cos_sum = lax.psum(loss[0, :2], "cell")
-    spot_sum = lax.psum(loss[1, :2], "spot")
-    losses = -cos_sum / G - spot_sum / loss[2, :2] + loss[3, :2]
-    grad_map = jnp.dot(gathered, full, precision=high) + cell_counts.astype(F32)[:, None] * vec[8][None, :]
-    grad_logits = exponent * (grad_map - column)
-    partial_grad = lax.dot_general(exponent, full, NT, precision=high, preferred_element_type=F32)
-    grad_expression = lax.psum_scatter(partial_grad, "spot", scatter_dimension=1, tiled=True)
-    return (losses, grad_logits, grad_expression)
+    grad_logits, grad_expression, losses, *_ = backward(
+        cfg, gp, gath, ehi, elo, vec, loss, cell_counts.astype(F32)[:, None]
+    )
+    return (losses[0, :2], grad_logits, grad_expression)
 
 
 def solution(mesh):

time: 607 us -> 521 us (0.86)
  Pallas kernels: 256 us -> 501 us
  waiting for transfers between devices: 206 us -> 0 us
  matrix products: 91.2 us -> 0 us
  blocking collectives: 22 us -> 0 us
  between operations: 14.1 us -> 0.65 us
    pallas_call x0 -> x1, Pallas kernels: none -> 245 us  [backward(): pl.pallas_call(functools.partial(backward_kernel, cfg), out_shape=(jax.Sh...]
    reduce_scatter x1 -> x0, waiting for transfers between devices: 111 us -> none  [local(): lax.psum_scatter(partial_grad, 'spot', scatter_dimension=1, tiled=True)]
    all_gather x1 -> x0, waiting for transfers between devices: 94.9 us -> none  [local(): full = lax.all_gather(gp, 'cell', axis=1).reshape(G, S)]
    dot_general x2 -> x0, matrix products: 91.2 us -> none  [the longest x1 47.9 us: local(): jnp.dot(gathered, full, precision=high)]
    psum x2 -> x0, blocking collectives: 22 us -> none  [the longest x1 11.8 us: local(): cos_sum = lax.psum(loss[0, :2], 'cell')]
    transpose x1 -> x0, local copies, waits for them, and re-layouts: 12 us -> none  [local(): gathered = gath.transpose(1, 0, 2).reshape(C, G)]
    unnamed x4, local copies, waits for them, and re-layouts: 0.66 us -> 12.4 us
  transfers between devices with their start and end apart: 2 -> 0, of which waited for: 2 -> 0; matrix products, arithmetic and copies ran while one was open for 10% -> 0% of each run, Pallas kernels for 0% -> 0%
where the time goes in v2:
time: 521 us; the launch traced here: 518 us
  Pallas kernels  501 us (96%)
  local copies, waits for them, and re-layouts  15.9 us (3%)
    pallas_call x1, Pallas kernels, forward(): pl.pallas_call(functools.partial(forward_kernel, cfg), out_shape=(jax.Sha...  255 us
    pallas_call x1, Pallas kernels, backward(): pl.pallas_call(functools.partial(backward_kernel, cfg), out_shape=(jax.Sh...  245 us
    unnamed x4, local copies, waits for them, and re-layouts  12.4 us

profile of v2, /device:TPU:9, one launch (start us, length us, event | category | flops | bytes accessed | tf_op | source)
XLA Modules:
  0.0 518.1 jit_solution(13741530053880461334)
XLA Ops:
  0.6 1.3 broadcast_in_dim.15.counts
  1.9 0.7 convert_element_type.3
  2.6 1.1 broadcast_in_dim.20.weight
  3.7 255.4 %forward.1 = (f32[16,1408,128]{2,1,0:T(8,128)}, bf16[1408,2048]{1,0:T(8,128)(2,1)}, bf16[1408,2048]{1,0:T(8,128)(2,1)}, f32[16,16,2048]{2,1,0:T(8,128)}, f32[16,2048]{1,0:T(8,128)}, /*index=5*/f32[8,128]{1,0:T(8,128)}) custom-call(f32[1408,2048]{1,0:T(8,128)} %logits.1, f32[1408,512]{1,0:T(8,128)} %expr.1, f32[256,2048]{1,0:T(8,128)} %spatial.1, ...), custom_call_target="tpu_custom_call" | custom-call | flops 35433480192 | bytes 23068672 | tf_op jit(solution)/shard_map/forward/pallas_call | solution.py:473
  259.1 245.4 %backward.1 = (f32[1408,2048]{1,0:T(8,128)}, f32[1408,512]{1,0:T(8,128)}, f32[8,128]{1,0:T(8,128)}, f32[16,8,16,2048]{3,2,1,0:T(8,128)}, f32[16,1408,128]{2,1,0:T(8,128)}, /*index=5*/f32[16,1408,128]{2,1,0:T(8,128)}) custom-call(f32[16,16,2048]{2,1,0:T(8,128)} %get-tuple-element.12.gp, f32[16,1408,128]{2,1,0:T(8,128)} %get-tuple-element.13.gath, ...), custom_call_target="tpu_custom_call" | custom-call | flops 70866960384 | bytes 46137344 | tf_op jit(solution)/shard_map/backward/pallas_call | solution.py:771
  504.6 1.2 slice_bitcast_fusion
  505.8 0.0 copy-start
  505.8 10.8 %copy.13 = f32[1408,2048]{1,0:T(8,128)} copy(f32[1408,2048]{1,0:T(8,128)} %get-tuple-element.25) | data formatting | bytes 23068672
  516.5 0.0 copy-done
  516.5 1.6 copy.14
Async XLA Ops:
  505.8 10.8 %copy-start = (f32[1408,512]{1,0:T(8,128)S(1)}, f32[1408,512]{1,0:T(8,128)}, u32[]{:S(2)}) copy-start(f32[1408,512]{1,0:T(8,128)} %get-tuple-element.26) | copy-start | bytes 8650756

commit v3 on v2

--- a/solution.py
+++ b/solution.py
@@ -86,7 +86,7 @@
     gath, ehi_out, elo_out, gp_out, vec_out, loss_out,
     ehi, elo, lbuf, stage, amat, partial, corer, half, chipr, pred, spat,
     tots, totr, acc, spots, spotr, gcol, gst, gstr, vec,
-    g_recv, up_send, down_send, l_sem, st_sem, core_send, core_recv, chip_send, chip_recv,
+    g_recv, up_send, down_send, l_sem, st_sem, put_sem, core_send, core_recv, chip_send, chip_recv,
     spat_send, spat_recv, tot_send, tot_recv, spot_send, spot_recv, gst_send, gst_recv, out_sem,
 ):
     cells, planes, C, S, G, GK, r = (cfg[k] for k in ("cells", "planes", "C", "S", "G", "GK", "r"))
@@ -121,7 +121,6 @@
         def _():
             z_copy(src, g, down, down_send).start()
 
-        pltpu.make_async_copy(src, gath.at[g], g_recv.at[g]).start()
         return 0
 
     lax.fori_loop(0, per, send_own, 0)
@@ -220,7 +219,17 @@
     def product(i):
         d, k = arrival(z, i, planes, per)
         g, slot = d * per + k, lax.rem(i, 2)
-        z_copy(gath.at[g], g, down, down_send).wait_recv()
+        own = pltpu.make_async_copy(expr.at[:, pl.ds(pl.multiple_of(k * GK, 128), GK)], stage, st_sem)
+        pull = pltpu.make_async_copy(gath.at[g], stage, st_sem)
+        put = pltpu.make_async_copy(stage, gath.at[g], put_sem)
+
+        @pl.when(d == z)
+        def _():
+            own.start()
+
+        @pl.when(d != z)
+        def _():
+            z_copy(gath.at[g], g, down, down_send).wait_recv()
 
         @pl.when((d < z) & (z < planes - 1))
         def _():
@@ -230,9 +239,15 @@
         def _():
             z_copy(gath.at[g], g, down, down_send).start()
 
-        pull = pltpu.make_async_copy(gath.at[g], stage, st_sem)
-        pull.start()
+        @pl.when(d != z)
+        def _():
+            pull.start()
+
         pull.wait()
+
+        @pl.when(d == z)
+        def _():
+            put.start()
 
         @pl.when(i >= 2)
         def _():
@@ -256,6 +271,10 @@
 
         lax.fori_loop(0, S // tile, multiply, 0)
         core_copy(g, slot).start()
+
+        @pl.when(d == z)
+        def _():
+            put.wait()
 
     def to_chips(i):
         d, k = arrival(z, i, planes, per)
@@ -464,7 +483,7 @@
         pltpu.VMEM((8, S), F32), pltpu.VMEM((cells, 8, S), F32), pltpu.VMEM((3, r, S), F32),
         pltpu.VMEM((8, S), F32), pltpu.VMEM((cells, 8, S), F32), pltpu.VMEM((wide, 128), F32),
         pltpu.VMEM((16, wide), F32), pltpu.VMEM((planes, 16, wide), F32), pltpu.VMEM((8, S), F32),
-        sem((chunks,)), sem((chunks,)), sem((chunks,)), sem((2,)), sem,
+        sem((chunks,)), sem((chunks,)), sem((chunks,)), sem((2,)), sem, sem,
         sem((2,)), sem((chunks,)), sem((2, chips)), sem((chunks, chips)),
         sem((blocks,)), sem((chunks,)), sem((cells,)), sem((cells,)), sem((cells,)), sem((cells,)),
         sem((planes,)), sem((planes,)), sem((3,)),
@@ -495,7 +514,7 @@
     cfg, gp, gath, ehi, elo, vec, loss, weight,
     grad_logits, grad_expr, losses, gpland, below, above,
     e2, x2, gph, gpl, gstage, xstage, zst, zsend, outst, cols, vecr, lossr,
-    e_sem, own_sem, gp_recv, own_send, fwd_send, gs_sem, xs_sem, b_recv, a_recv, zs_sem, zst_sem, out_sem,
+    e_sem, gp_recv, own_send, fwd_send, gs_sem, xs_sem, b_recv, a_recv, zs_sem, zst_sem, out_sem,
     vec_send, vec_recv, loss_send, loss_recv,
 ):
     cells, planes, C, S, G, GK, r = (cfg[k] for k in ("cells", "planes", "C", "S", "G", "GK", "r"))
@@ -547,7 +566,6 @@
             return 0
 
         lax.fori_loop(1, chips + 1, start, 0)
-        pltpu.make_async_copy(gp.at[g], gpland.at[g, c], own_sem.at[g]).start()
 
     send_own(0)
     send_own(1)
@@ -570,23 +588,23 @@
 
         x_copy = pltpu.make_async_copy(gath.at[g], xstage, xs_sem)
         x_copy.start()
+        pltpu.make_async_copy(gp.at[g], gstage.at[c], gs_sem).start()
 
         def pass_on(step, _):
             other = lax.rem(chip + step, chips)
             landed(g, 2 * other + core)
             forward_copy(g, other).start()
+            pltpu.make_async_copy(gpland.at[g, 2 * other + core], gstage.at[2 * other + core], gs_sem).start()
             return 0
 
         lax.fori_loop(1, chips, pass_on, 0)
 
         def take(other, _):
             landed(g, 2 * other + 1 - core)
+            pltpu.make_async_copy(gpland.at[g, 2 * other + 1 - core], gstage.at[2 * other + 1 - core], gs_sem).start()
             return 0
 
         lax.fori_loop(0, chips, take, 0)
-        pltpu.make_async_copy(gp.at[g], gpland.at[g, c], own_sem.at[g]).wait()
-        g_copy = pltpu.make_async_copy(gpland.at[g], gstage, gs_sem)
-        g_copy.start()
         x_copy.wait()
         columns = pl.ds(pl.multiple_of(g * GK, 128), GK)
 
@@ -597,7 +615,7 @@
             return 0
 
         lax.fori_loop(0, parts, split_x, 0)
-        g_copy.wait()
+        pltpu.make_async_copy(gstage, gstage, gs_sem).wait()
 
         def split_g(t, _):
             place = pl.ds(pl.multiple_of(t * 128, 128), 128)
@@ -764,7 +782,7 @@
         pltpu.VMEM((cells, r, S), F32), pltpu.VMEM((C, GK), F32), pltpu.VMEM((C, GK), F32),
         pltpu.VMEM((3, C, GK), F32), pltpu.VMEM((2, rows, tile), F32),
         pltpu.VMEM((8, S), F32), pltpu.VMEM((cells, 8, S), F32), pltpu.VMEM((planes, 8, 128), F32),
-        sem((2, parts)), sem((chunks,)), sem((chunks, cells)), sem((chunks, chips)), sem((chunks, chips)),
+        sem((2, parts)), sem((chunks, cells)), sem((chunks, chips)), sem((chunks, chips)),
         sem, sem, sem((chunks,)), sem((chunks,)), sem((3,)), sem, sem((2,)),
         sem((cells,)), sem((cells,)), sem((planes,)), sem((planes,)),
     ]

time: 521 us -> 480 us (0.921)
  Pallas kernels: 501 us -> 461 us
    pallas_call x1, Pallas kernels: 255 us -> 220 us  [forward(): pl.pallas_call(functools.partial(forward_kernel, cfg), out_shape=(jax.Sha...]
where the time goes in v3:
time: 480 us; the launch traced here: 478 us
  Pallas kernels  461 us (96%)
  local copies, waits for them, and re-layouts  15.9 us (3%)
    pallas_call x1, Pallas kernels, backward(): pl.pallas_call(functools.partial(backward_kernel, cfg), out_shape=(jax.Sh...  241 us
    pallas_call x1, Pallas kernels, forward(): pl.pallas_call(functools.partial(forward_kernel, cfg), out_shape=(jax.Sha...  220 us
    unnamed x4, local copies, waits for them, and re-layouts  12.4 us

profile of v3, /device:TPU:9, one launch (start us, length us, event | category | flops | bytes accessed | tf_op | source)
XLA Modules:
  0.0 477.8 jit_solution(8540816942555648308)
XLA Ops:
  0.6 1.3 broadcast_in_dim.15.counts
  1.9 0.7 convert_element_type.3
  2.6 1.1 broadcast_in_dim.20.weight
  3.7 219.6 %forward.1 = (f32[16,1408,128]{2,1,0:T(8,128)}, bf16[1408,2048]{1,0:T(8,128)(2,1)}, bf16[1408,2048]{1,0:T(8,128)(2,1)}, f32[16,16,2048]{2,1,0:T(8,128)}, f32[16,2048]{1,0:T(8,128)}, /*index=5*/f32[8,128]{1,0:T(8,128)}) custom-call(f32[1408,2048]{1,0:T(8,128)} %logits.1, f32[1408,512]{1,0:T(8,128)} %expr.1, f32[256,2048]{1,0:T(8,128)} %spatial.1, ...), custom_call_target="tpu_custom_call" | custom-call | flops 35433480192 | bytes 23068672 | tf_op jit(solution)/shard_map/forward/pallas_call | solution.py:492
  223.3 240.9 %backward.1 = (f32[1408,2048]{1,0:T(8,128)}, f32[1408,512]{1,0:T(8,128)}, f32[8,128]{1,0:T(8,128)}, f32[16,8,16,2048]{3,2,1,0:T(8,128)}, f32[16,1408,128]{2,1,0:T(8,128)}, /*index=5*/f32[16,1408,128]{2,1,0:T(8,128)}) custom-call(f32[16,16,2048]{2,1,0:T(8,128)} %get-tuple-element.12.gp, f32[16,1408,128]{2,1,0:T(8,128)} %get-tuple-element.13.gath, ...), custom_call_target="tpu_custom_call" | custom-call | flops 70866960384 | bytes 46137344 | tf_op jit(solution)/shard_map/backward/pallas_call | solution.py:789
  464.3 1.2 slice_bitcast_fusion
  465.5 0.0 copy-start
  465.5 10.8 %copy.13 = f32[1408,2048]{1,0:T(8,128)} copy(f32[1408,2048]{1,0:T(8,128)} %get-tuple-element.25) | data formatting | bytes 23068672
  476.3 0.0 copy-done
  476.3 1.6 copy.14
Async XLA Ops:
  465.5 10.8 %copy-start = (f32[1408,512]{1,0:T(8,128)S(1)}, f32[1408,512]{1,0:T(8,128)}, u32[]{:S(2)}) copy-start(f32[1408,512]{1,0:T(8,128)} %get-tuple-element.26) | copy-start | bytes 8650756

commit v4 on v1

--- a/solution.py
+++ b/solution.py
@@ -83,15 +83,16 @@
 
 def forward_kernel(
     cfg, logits, expr, spatial, counts, dens, slide, pad,
-    gath, ehi_out, elo_out, gp_out, vec_out, loss_out,
-    ehi, elo, lbuf, stage, amat, partial, corer, half, chipr, pred, spat,
+    gath, ehi_out, elo_out, x_out, far_logits, gp_out, vec_out, loss_out,
+    ehi, elo, lbuf, stage, xparts, amat, partial, corer, half, chipr, pred, spat,
     tots, totr, acc, spots, spotr, gcol, gst, gstr, vec,
-    g_recv, up_send, down_send, l_sem, st_sem, core_send, core_recv, chip_send, chip_recv,
-    spat_send, spat_recv, tot_send, tot_recv, spot_send, spot_recv, gst_send, gst_recv, out_sem,
+    g_recv, up_send, down_send, l_sem, st_sem, put_sem, core_send, core_recv, chip_send, chip_recv,
+    far_send, far_recv, spat_send, spat_recv, tot_send, tot_recv, spot_send, spot_recv, gst_send, gst_recv, out_sem,
 ):
     cells, planes, C, S, G, GK, r = (cfg[k] for k in ("cells", "planes", "C", "S", "G", "GK", "r"))
     chips, per, chunks = cells // 2, G // planes // GK, G // GK
-    rows, tile = cfg["rows"], cfg["tile"]
+    rows, tile, parts, helped = cfg["rows"], cfg["tile"], cfg["parts"], cfg["helped"]
+    part, pieces = C // parts, cfg["pieces"]
     own_genes = G // cells
     c, z = lax.axis_index("cell"), lax.axis_index("spot")
     chip, core = lax.div(c, 2), lax.rem(c, 2)
@@ -121,10 +122,21 @@
         def _():
             z_copy(src, g, down, down_send).start()
 
-        pltpu.make_async_copy(src, gath.at[g], g_recv.at[g]).start()
         return 0
 
     lax.fori_loop(0, per, send_own, 0)
+
+    at_end = (z == 0) | (z == planes - 1)
+    helper = ((z == 1) | (z == planes - 2)) & helped
+    beside = jnp.where(z == 0, 1, jnp.where(z == planes - 1, planes - 2, jnp.where(z == 1, 0, planes - 1)))
+    piece = C // 2 // pieces
+
+    def far_copy(n):
+        return pltpu.make_async_remote_copy(
+            src_ref=logits.at[pl.ds(pl.multiple_of(C // 2 + n * piece, 8), piece)],
+            dst_ref=far_logits.at[pl.ds(pl.multiple_of(n * piece, 8), piece)],
+            send_sem=far_send.at[n], recv_sem=far_recv.at[n], device_id=(c, beside), device_id_type=MESH,
+        )
 
     blocks = own_genes // r
 
@@ -220,7 +232,16 @@
     def product(i):
         d, k = arrival(z, i, planes, per)
         g, slot = d * per + k, lax.rem(i, 2)
-        z_copy(gath.at[g], g, down, down_send).wait_recv()
+        own = pltpu.make_async_copy(expr.at[:, pl.ds(pl.multiple_of(k * GK, 128), GK)], stage, st_sem)
+        pull = pltpu.make_async_copy(gath.at[g], stage, st_sem)
+
+        @pl.when(d == z)
+        def _():
+            own.start()
+
+        @pl.when(d != z)
+        def _():
+            z_copy(gath.at[g], g, down, down_send).wait_recv()
 
         @pl.when((d < z) & (z < planes - 1))
         def _():
@@ -230,9 +251,25 @@
         def _():
             z_copy(gath.at[g], g, down, down_send).start()
 
-        pull = pltpu.make_async_copy(gath.at[g], stage, st_sem)
-        pull.start()
+        @pl.when(d != z)
+        def _():
+            pull.start()
+
         pull.wait()
+        columns = pl.ds(pl.multiple_of(g * GK, 128), GK)
+
+        @pl.when(i >= 1)
+        def _():
+            pltpu.make_async_copy(xparts, x_out.at[:, :, columns], put_sem).wait()
+
+        def keep_parts(t, _):
+            high, low = split(stage[pl.ds(pl.multiple_of(t * part, 16), part), :])
+            xparts[t, pl.ds(0, part), :] = high
+            xparts[t, pl.ds(part, part), :] = low
+            return 0
+
+        lax.fori_loop(0, parts, keep_parts, 0)
+        pltpu.make_async_copy(xparts, x_out.at[:, :, columns], put_sem).start()
 
         @pl.when(i >= 2)
         def _():
@@ -307,6 +344,10 @@
         gcol[pl.ds(pl.multiple_of(g * r, 8), r), :] = cols
 
     def step(i, _):
+        @pl.when((i >= per) & (i < per + pieces) & at_end & helped)
+        def _():
+            far_copy(i - per).start()
+
         @pl.when(i < chunks)
         def _():
             product(i)
@@ -392,21 +433,36 @@
         return 0
 
     lax.fori_loop(0, chunks, gradient, 0)
-    copy = pltpu.make_async_copy(pred, gp_out, out_sem.at[2])
+    copy = pltpu.make_async_copy(pred, gp_out.at[:, chip, core], out_sem.at[2])
     copy.start()
     vec_out[...] = jnp.zeros_like(vec_out)
     vec_out[0:1, :] = jnp.sum(acc[0], axis=0, keepdims=True)
     vec_out[8:9, :] = vec[6:7, :]
     vec_out[9:10, :] = vec[7:8, :]
     lane = lax.broadcasted_iota(jnp.int32, (1, 128), 1)
+    vec_out[1:2, 0:128] = jnp.where(lane == 0, cos_sums[0], jnp.where(lane == 1, cos_sums[1], 0.0))
     spot_sums = [jnp.sum(vec[4 + m : 5 + m, :] * spot_cos, axis=1, keepdims=True) for m in range(2)]
     loss_out[...] = jnp.zeros_like(loss_out)
-    for n, v in enumerate((cos_sums, spot_sums, live, divergence)):
+    for n, v in enumerate((spot_sums, live, divergence)):
         loss_out[n : n + 1, :] = jnp.where(lane == 0, v[0], jnp.where(lane == 1, v[1], 0.0))
 
     copy.wait()
     for copy in keep:
         copy.wait()
+    pltpu.make_async_copy(xparts, x_out.at[:, :, pl.ds(0, GK)], put_sem).wait()
+
+    def drain_far(n, _):
+        @pl.when(at_end & helped)
+        def _():
+            far_copy(n).wait_send()
+
+        @pl.when(helper)
+        def _():
+            far_copy(n).wait_recv()
+
+        return 0
+
+    lax.fori_loop(0, pieces, drain_far, 0)
 
     def drain_z(g, _):
         d = lax.div(g, per)
@@ -456,15 +512,16 @@
     sem = pltpu.SemaphoreType.DMA
     scratch = [
         pltpu.VMEM((C, S), BF16), pltpu.VMEM((C, S), BF16), pltpu.VMEM((2, rows, S), F32),
-        pltpu.VMEM((C, GK), F32), pltpu.VMEM((2 * GK, C), BF16),
+        pltpu.VMEM((C, GK), F32), pltpu.VMEM((cfg["parts"], 2 * C // cfg["parts"], GK), BF16), pltpu.VMEM((2 * GK, C), BF16),
         pltpu.VMEM((2, chips, 2, r, S), F32), pltpu.VMEM((chunks, chips, r, S), F32),
         pltpu.VMEM((2, chips, r, S), F32), pltpu.VMEM((chunks, chips, r, S), F32),
         pltpu.VMEM((chunks, r, S), F32), pltpu.VMEM((chunks, r, S), F32),
         pltpu.VMEM((8, S), F32), pltpu.VMEM((cells, 8, S), F32), pltpu.VMEM((3, r, S), F32),
         pltpu.VMEM((8, S), F32), pltpu.VMEM((cells, 8, S), F32), pltpu.VMEM((wide, 128), F32),
         pltpu.VMEM((16, wide), F32), pltpu.VMEM((planes, 16, wide), F32), pltpu.VMEM((8, S), F32),
-        sem((chunks,)), sem((chunks,)), sem((chunks,)), sem((2,)), sem,
+        sem((chunks,)), sem((chunks,)), sem((chunks,)), sem((2,)), sem, sem,
         sem((2,)), sem((chunks,)), sem((2, chips)), sem((chunks, chips)),
+        sem((cfg["pieces"],)), sem((cfg["pieces"],)),
         sem((blocks,)), sem((chunks,)), sem((cells,)), sem((cells,)), sem((cells,)), sem((cells,)),
         sem((planes,)), sem((planes,)), sem((3,)),
     ]
@@ -475,12 +532,14 @@
             jax.ShapeDtypeStruct((chunks, C, GK), F32),
             jax.ShapeDtypeStruct((C, S), BF16),
             jax.ShapeDtypeStruct((C, S), BF16),
-            jax.ShapeDtypeStruct((chunks, r, S), F32),
+            jax.ShapeDtypeStruct((cfg["parts"], 2 * C // cfg["parts"], G), BF16),
+            jax.ShapeDtypeStruct((C // 2, S), F32),
+            jax.ShapeDtypeStruct((chunks, chips, 2, r, S), F32),
             jax.ShapeDtypeStruct((16, S), F32),
             jax.ShapeDtypeStruct((8, 128), F32),
         ),
         in_specs=[ANY, ANY, ANY, VMEM, VMEM, VMEM, VMEM],
-        out_specs=(ANY, ANY, ANY, ANY, VMEM, VMEM),
+        out_specs=(ANY, ANY, ANY, ANY, ANY, ANY, VMEM, VMEM),
         scratch_shapes=scratch,
         compiler_params=pltpu.CompilerParams(
             collective_id=0, has_side_effects=True, vmem_limit_bytes=56 * 2**20
@@ -490,28 +549,622 @@
     )(logits, expression, spatial, counts, dens, slide, pad)
 
 
+def backward_kernel(
+    cfg, ehi, elo, xparts, far_logits, vec, loss, counts, _gp, _gath,
+    grad_logits, grad_expr, losses, land, far_land, zland, zlast,
+    e2, x2, e3, gph, gpl, far_g, gstage, fstage, lbuf, zst, zsend, outst, inst, cols, vecr, lossr, weight,
+    e_sem, x_sem, l_sem, g_recv, g_pair, g_sent, f_recv, f_pair, f_sent, row_recv, row_sent, gs_sem, fs_sem,
+    z_recv, zs_sem, zst_sem, out_sem, in_sem, vec_send, vec_recv, loss_send, loss_recv,
+):
+    cells, planes, C, S, G, GK, r = (cfg[k] for k in ("cells", "planes", "C", "S", "G", "GK", "r"))
+    chips, per, chunks = cells // 2, G // planes // GK, G // GK
+    parts, tile, slots, group, zslots = (cfg[k] for k in ("parts", "tile", "slots", "group", "zslots"))
+    ahead = cfg["ahead"]
+    handed = cfg["handed"]
+    count, groups = parts * (S // tile), chunks // group
+    cuts = (0, chunks // 2, chunks)
+    last = len(cuts) - 2
+    helped, across = cfg["helped"], cfg["across"]
+    rows, tiles, halves = C // parts, S // tile, parts // 2
+    piece = cfg["piece"]
+    pieces = C // 2 // piece
+    down_chips = chips // across
+    c, z = lax.axis_index("cell"), lax.axis_index("spot")
+    chip, core = lax.div(c, 2), lax.rem(c, 2)
+    chip_row, chip_col = lax.div(chip, across), lax.rem(chip, across)
+    sibling = c + 1 - 2 * core
+    in_plane = lambda other: (other, z)
+    in_column = lambda other: (c, other)
+    at_end = ((z == 0) | (z == planes - 1)) & helped
+    helper = ((z == 1) | (z == planes - 2)) & helped
+    beside = jnp.where(z == 0, 1, jnp.where(z == planes - 1, planes - 2, jnp.where(z == 1, 0, planes - 1)))
+
+    def order(i):
+        d, k = arrival(z, chunks - 1 - i, planes, per)
+        return d, k, d * per + k
+
+    greet(c, z, cells, planes)
+
+    def spread(land, recv, pair, sent, buffer, ready):
+        def copy(ref, source, g, other):
+            return pltpu.make_async_remote_copy(
+                src_ref=ref, dst_ref=ref, send_sem=sent.at[g, 0], recv_sem=recv.at[g, source],
+                device_id=(2 * other + core, z), device_id_type=MESH,
+            )
+
+        def along_row(n):
+            return chip_row * across + lax.rem(chip_col + n, across)
+
+        def along_col(n):
+            return lax.rem(chip_row + n, down_chips) * across + chip_col
+
+        def each(count, body):
+            def one(n, _):
+                body(n)
+                return 0
+
+            lax.fori_loop(1, count, one, 0)
+
+        def send(g):
+            own = land.at[g, chip, core]
+            each(across, lambda n: copy(own, chip, g, along_row(n)).start())
+            each(down_chips, lambda n: copy(own, chip, g, along_col(n)).start())
+
+        def landed(g, source):
+            ref = land.at[g, source, core]
+            pltpu.make_async_copy(ref, ref, recv.at[g, source]).wait()
+
+        def first_hop(g):
+            def from_row(n):
+                source = along_row(n)
+                landed(g, source)
+                half = land.at[g, source, core, :, pl.ds(0, S // 2)]
+                each(down_chips, lambda m: copy(half, source, g, along_col(m)).start())
+
+            def from_col(n):
+                source = along_col(n)
+                landed(g, source)
+                half = land.at[g, source, core, :, pl.ds(S // 2, S // 2)]
+                each(across, lambda m: copy(half, source, g, along_row(m)).start())
+
+            each(across, from_row)
+            each(down_chips, from_col)
+
+        def to_sibling(g):
+            ref = land.at[g, :, core]
+            return pltpu.make_async_remote_copy(
+                src_ref=ref, dst_ref=ref, send_sem=sent.at[g, 1], recv_sem=pair.at[g],
+                device_id=(sibling, z), device_id_type=MESH,
+            )
+
+        def second_hop(g):
+            def from_rest(n):
+                other = lax.rem(chip_row + 1 + lax.div(n - 1, across - 1), down_chips) * across
+                landed(g, other + lax.rem(chip_col + 1 + lax.rem(n - 1, across - 1), across))
+
+            each((across - 1) * (down_chips - 1) + 1, from_rest)
+            to_sibling(g).start()
+
+        def stage(g, slot):
+            ref = land.at[g, :, 1 - core]
+            pltpu.make_async_copy(ref, ref, pair.at[g]).wait()
+            pltpu.make_async_copy(land.at[g], buffer.at[slot], ready.at[slot]).start()
+
+        def take(slot, high_ref, low_ref, first):
+            pltpu.make_async_copy(buffer.at[slot], buffer.at[slot], ready.at[slot]).wait()
+
+            def split_tile(t, _):
+                place = pl.ds(pl.multiple_of(t * 128, 128), 128)
+                high, low = split(buffer[slot, :, :, :, place].reshape(GK, 128))
+                lines = pl.ds(pl.multiple_of(first, 128), GK)
+                high_ref[lines, place] = high
+                low_ref[lines, place] = low
+                return 0
+
+            lax.fori_loop(0, S // 128, split_tile, 0)
+
+        def drain(g):
+            direct = land.at[g, pl.ds(0, chips - 1), 0]
+            pltpu.make_async_copy(direct, direct, sent.at[g, 0]).wait()
+            to_sibling(g).wait_send()
+
+        return send, first_hop, second_hop, stage, take, drain
+
+    send_own, first_own, second_own, stage_own, take_own, drain_own = spread(
+        land, g_recv, g_pair, g_sent, gstage, gs_sem
+    )
+    send_far, first_far, second_far, stage_far, take_far, drain_far = spread(
+        far_land, f_recv, f_pair, f_sent, fstage, fs_sem
+    )
+
+    def rank(d, k):
+        end = jnp.where(at_end, z, beside)
+        return (planes - 1 - jnp.abs(d - end)) * per + per - 1 - k
+
+    def row_copy(n, g):
+        return pltpu.make_async_remote_copy(
+            src_ref=land.at[g, chip, core], dst_ref=far_land.at[n, chip, core],
+            send_sem=row_sent.at[n], recv_sem=row_recv.at[n],
+            device_id=(c, beside), device_id_type=MESH,
+        )
+
+    def announce(i):
+        _, _, g = order(i)
+        send_own(g)
+
+        @pl.when(at_end & (i < handed))
+        def _():
+            row_copy(i, g).start()
+
+    announce(0)
+    announce(1)
+
+    def e_copy(t):
+        place = pl.ds(pl.multiple_of(t * rows, 16), rows)
+        return (
+            pltpu.make_async_copy(ehi.at[place], e2.at[t, pl.ds(0, rows)], e_sem.at[0, t]),
+            pltpu.make_async_copy(elo.at[place], e2.at[t, pl.ds(rows, rows)], e_sem.at[1, t]),
+        )
+
+    for t in range(parts):
+        for copy in e_copy(t):
+            copy.start()
+    def load_x(i, _):
+        from_place = pl.ds(pl.multiple_of(order(i)[2] * GK, 128), GK)
+        to_place = pl.ds(pl.multiple_of(i * GK, 128), GK)
+        pltpu.make_async_copy(xparts.at[:, :, from_place], x2.at[:, :, to_place], x_sem).start()
+        return 0
+
+    mine = vec.at[pl.ds(0, 8)]
+    share(mine, vecr, vec_send, vec_recv, c, cells, in_plane)
+    share(loss, lossr, loss_send, loss_recv, z, planes, in_column)
+
+    def far_exponentials():
+        def load(n):
+            return pltpu.make_async_copy(
+                far_logits.at[pl.ds(pl.multiple_of(n * piece, 8), piece)], lbuf.at[lax.rem(n, 2)], l_sem.at[lax.rem(n, 2)]
+            )
+
+        for n in range(2):
+            load(n).start()
+
+        def exps(n, _):
+            load(n).wait()
+            high, low = split(jnp.exp(lbuf[lax.rem(n, 2)]))
+            t, place = lax.div(n * piece, rows), lax.rem(n * piece, rows)
+            e3[t, pl.ds(pl.multiple_of(place, 16), piece), :] = high
+            e3[t, pl.ds(pl.multiple_of(rows + place, 16), piece), :] = low
+
+            @pl.when(n + 2 < pieces)
+            def _():
+                load(n + 2).start()
+
+            return 0
+
+        lax.fori_loop(0, pieces, exps, 0)
+
+    def far_step(n, what):
+        @pl.when(helper & (n < handed))
+        def _():
+            what(n)
+
+    def ask_far(n):
+        row_copy(n, 0).wait_recv()
+        send_far(n)
+
+    def z_copy(land, index, number, slot, n, h, to):
+        place = pl.ds(h * (C // 2), C // 2)
+        return pltpu.make_async_remote_copy(
+            src_ref=zsend.at[slot, n, h], dst_ref=land.at[index, place], send_sem=zs_sem.at[slot, n, h],
+            recv_sem=z_recv.at[number, h], device_id=(c, to), device_id_type=MESH,
+        )
+
+    def sent(slot, n, h):
+        pltpu.make_async_copy(zsend.at[slot, n, h], zsend.at[slot, n, h], zs_sem.at[slot, n, h]).wait()
+
+    def had(p, h):
+        return True if h == 0 else jnp.logical_not(at_end) | (p * group >= handed)
+
+    def multiply_group(p):
+        slot = lax.rem(p, zslots)
+        lines = pl.ds(pl.multiple_of(p * group * GK, 128), group * GK)
+
+        def half(h):
+            @pl.when((p >= zslots) & had(p - zslots, h))
+            def _():
+                for n in range(group):
+                    sent(slot, n, h)
+
+            def multiply(t, _):
+                both = dot(e2[h * halves + t], gph[lines, :], NT)
+                total = both[:rows] + both[rows:] + dot(e2[h * halves + t, pl.ds(0, rows)], gpl[lines, :], NT)
+                for n in range(group):
+                    zsend[slot, n, h, pl.ds(pl.multiple_of(t * rows, 16), rows), :] = total[:, n * GK : (n + 1) * GK]
+                return 0
+
+            lax.fori_loop(0, halves, multiply, 0)
+
+        half(0)
+
+        @pl.when(had(p, 1))
+        def _():
+            half(1)
+
+    def finish_group(p):
+        slot = lax.rem(p, zslots)
+        members = [order(p * group + n) for n in range(group)]
+
+        def first(h):
+            for n, (d, k, g) in enumerate(members):
+                fetch_half(n, h, d, k, g)
+
+        def second(h):
+            for n, (d, k, g) in enumerate(members):
+                finish_half(slot, n, h, d, k, g)
+
+        first(0)
+
+        @pl.when(had(p, 1))
+        def _():
+            first(1)
+
+        second(0)
+
+        @pl.when(had(p, 1))
+        def _():
+            for n, (d, k, g) in enumerate(members):
+
+                @pl.when(helper & (rank(d, k) < handed))
+                def _():
+                    take_far(n, far_g.at[0], far_g.at[1], 0)
+
+                    def more(t, _):
+                        right = jnp.concatenate([far_g[0], far_g[1]], axis=0)
+                        both = dot(e3[t, pl.ds(0, rows)], right, NT)
+                        total = both[:, :GK] + both[:, GK:] + dot(e3[t, pl.ds(rows, rows)], far_g[0], NT)
+                        zsend[slot, n, 1, pl.ds(pl.multiple_of(t * rows, 16), rows), :] += total
+                        return 0
+
+                    lax.fori_loop(0, halves, more, 0)
+
+            second(1)
+
+    def fetch(land, index, number, n, h):
+        place = land.at[index, pl.ds(h * (C // 2), C // 2)]
+        pltpu.make_async_copy(place, place, z_recv.at[number, h]).wait()
+        copy = pltpu.make_async_copy(place, zst.at[n, h], zst_sem.at[n, h])
+        copy.start()
+        return copy
+
+    def from_behind(h, d, k):
+        comes = ((d >= z) & (z > 0)) | ((d < z) & (z < planes - 1))
+        if h == 0:
+            return comes
+        from_end = ((z == 1) & (d >= z)) | ((z == planes - 2) & (d < z))
+        return comes & jnp.logical_not(helper & from_end & (rank(d, k) < handed))
+
+    def from_front(h, d, k):
+        comes = (d == z) & (z < planes - 1)
+        if h == 0:
+            return comes
+        return comes & jnp.logical_not(helper & (z == planes - 2) & (rank(d, k) < handed))
+
+    def fetch_half(n, h, d, k, g):
+        @pl.when(from_behind(h, d, k))
+        def _():
+            fetch(zland, g, g, n, h)
+
+    def finish_half(slot, n, h, d, k, g):
+        def add():
+            pltpu.make_async_copy(zst.at[n, h], zst.at[n, h], zst_sem.at[n, h]).wait()
+
+            def one(t, _):
+                place = pl.ds(pl.multiple_of(t * rows, 16), rows)
+                zsend[slot, n, h, place, :] += zst[n, h, place, :]
+                return 0
+
+            lax.fori_loop(0, halves, one, 0)
+
+        @pl.when(from_behind(h, d, k))
+        def _():
+            add()
+
+        @pl.when(from_front(h, d, k))
+        def _():
+            fetch(zlast, k, chunks + k, n, h)
+            add()
+
+        @pl.when(d > z)
+        def _():
+            z_copy(zland, g, g, slot, n, h, jnp.minimum(z + 1, planes - 1)).start()
+
+        @pl.when(d < z - 1)
+        def _():
+            z_copy(zland, g, g, slot, n, h, jnp.maximum(z - 1, 0)).start()
+
+        @pl.when(d == z - 1)
+        def _():
+            z_copy(zlast, k, chunks + k, slot, n, h, jnp.maximum(z - 1, 0)).start()
+
+        @pl.when(d == z)
+        def _():
+            place = pl.ds(h * (C // 2), C // 2), pl.ds(pl.multiple_of(k * GK, 128), GK)
+            pltpu.make_async_copy(zsend.at[slot, n, h], grad_expr.at[place], zs_sem.at[slot, n, h]).start()
+
+    def tile_of(j):
+        t, n = lax.div(j, tiles), lax.rem(j, tiles)
+        return grad_logits.at[pl.ds(pl.multiple_of(t * rows, 8), rows), pl.ds(pl.multiple_of(n * tile, 128), tile)]
+
+    def out_copy(j):
+        return pltpu.make_async_copy(outst.at[lax.rem(j, 2)], tile_of(j), out_sem.at[lax.rem(j, 2)])
+
+    def in_copy(j):
+        return pltpu.make_async_copy(tile_of(j), inst.at[lax.rem(j, 2)], in_sem.at[lax.rem(j, 2)])
+
+    def map_part(j, first, last):
+        t, place = lax.div(j, tiles), pl.ds(pl.multiple_of(lax.rem(j, tiles) * tile, 128), tile)
+        genes = pl.ds(first * GK, (last - first) * GK)
+        both = dot(x2[t, :, genes], gph[genes, place])
+        return both[:rows] + both[rows:] + dot(x2[t, pl.ds(0, rows), genes], gpl[genes, place])
+
+    def stored_part(j, stage):
+        slot = lax.rem(j, 2)
+
+        @pl.when(j >= 2)
+        def _():
+            out_copy(j - 2).wait()
+
+        if stage > 0:
+
+            @pl.when(j + 1 < count)
+            def _():
+                in_copy(j + 1).start()
+
+        total = map_part(j, cuts[stage], cuts[stage + 1])
+        if stage == last:
+            t, place = lax.div(j, tiles), pl.ds(pl.multiple_of(lax.rem(j, tiles) * tile, 128), tile)
+            scale = weight[pl.ds(pl.multiple_of(t * rows, 8), rows), 0:1]
+            total = total + (scale * cols[0:1, place] - cols[1:2, place])
+        if stage > 0:
+            in_copy(j).wait()
+            total = total + inst[slot]
+        if stage == last:
+            exponent = e2[t, pl.ds(0, rows), place].astype(F32) + e2[t, pl.ds(rows, rows), place].astype(F32)
+            total = exponent * total
+        outst[slot] = total
+        out_copy(j).start()
+
+    ends = [0] + [group - 1 + 2 * group * p for p in range(1, groups)]
+    finishes = [4 + group + 2 * group * p for p in range(groups)]
+    makes = [max((p + 1) * group - 1, finishes[p - zslots] + 5 if p >= zslots else 0) for p in range(groups)]
+    makes = finishes
+
+    def at(t, of_ends, of_others):
+        p = jnp.int32(-1)
+        for n in range(groups):
+            p = jnp.where(t == jnp.where(at_end, of_ends[n], of_others[n]), n, p)
+        return p
+
+    def step(t, _):
+        def hops(firsts, seconds):
+            for i in firsts:
+                first_own(order(i)[2])
+            for i in seconds:
+                second_own(order(i)[2])
+
+        @pl.when(t == 0)
+        def _():
+            hops((0, 1), ())
+            for i in range(2, ahead + 1):
+                announce(i)
+            hops((), (0, 1))
+            stage_own(order(0)[2], 0)
+            stage_own(order(1)[2], 1)
+
+        @pl.when(t == 1)
+        def _():
+            hops((2, 3), (2,))
+
+        @pl.when(t == 2)
+        def _():
+            hops((4, 5), (3, 4))
+
+        @pl.when((t >= 3) & (t + 3 < chunks))
+        def _():
+            first_own(order(t + 3)[2])
+
+        @pl.when((t >= 3) & (t + 2 < chunks))
+        def _():
+            second_own(order(t + 2)[2])
+
+        @pl.when((t >= 1) & (t + 1 < chunks))
+        def _():
+            stage_own(order(t + 1)[2], lax.rem(t + 1, 2))
+
+        @pl.when((t >= 1) & (t + ahead < chunks))
+        def _():
+            announce(t + ahead)
+
+        @pl.when(lax.rem(t, 2) == 0)
+        def _():
+            far_step(lax.div(t, 2), ask_far)
+
+            @pl.when(t >= 2)
+            def _():
+                far_step(lax.div(t - 2, 2), first_far)
+
+        @pl.when((t >= 3) & (lax.rem(t, 2) == 1))
+        def _():
+            far_step(lax.div(t - 3, 2), second_far)
+
+        soon = at(t + 1, [-1] * groups, finishes)
+
+        @pl.when(helper & (soon >= 0))
+        def _():
+            for n in range(group):
+                d, k, _ = order(soon * group + n)
+                far_step(rank(d, k), lambda m, n=n: stage_far(m, n))
+
+        @pl.when((t < chunks) & (t != 1))
+        def _():
+            take_own(lax.rem(t, 2), gph, gpl, t * GK)
+
+        @pl.when(t == 0)
+        def _():
+            take_own(1, gph, gpl, GK)
+            for n in range(parts):
+                for copy in e_copy(n):
+                    copy.wait()
+            lax.fori_loop(0, chunks, load_x, 0)
+
+        p = at(t, ends, makes)
+
+        @pl.when(p >= 0)
+        def _():
+            multiply_group(p)
+
+        q = at(t, ends, finishes)
+
+        @pl.when(q >= 0)
+        def _():
+            finish_group(q)
+
+        @pl.when((t == 2) & helper)
+        def _():
+            far_exponentials()
+
+        @pl.when(t == cuts[1])
+        def _():
+            pltpu.make_async_copy(xparts, x2, x_sem).wait()
+            total = collect(mine, vecr, vec_send, vec_recv, c, cells, in_plane)
+            spot_sum = collect(loss, lossr, loss_send, loss_recv, z, planes, in_column)
+            weight[...] = jnp.broadcast_to(counts[...].astype(F32), (128, C)).T
+            cols[0:1, :] = vec[8:9, :]
+            cols[1:2, :] = total[0:1, :] + vec[9:10, :]
+            losses[...] = jnp.zeros_like(losses)
+            losses[0:1, :] = loss[2:3, :] - total[1:2, 0:128] / G - spot_sum[0:1, :] / loss[1:2, :]
+
+        for stage in range(last + 1):
+            begin = cuts[stage + 1]
+            steps = cuts[stage + 2] - begin if stage < last else count
+            each = -(-count // steps)
+
+            @pl.when((t >= begin) & (t < begin + steps))
+            def _():
+                if stage > 0:
+
+                    @pl.when(t == begin)
+                    def _():
+                        for j in range(count - 2, count):
+                            out_copy(j).wait()
+                        in_copy(0).start()
+
+                def one(j, _):
+                    stored_part(j, stage)
+                    return 0
+
+                lax.fori_loop(
+                    jnp.minimum((t - begin) * each, count), jnp.minimum((t - begin + 1) * each, count), one, 0
+                )
+
+        return 0
+
+    lax.fori_loop(0, slots, step, 0)
+
+    for p in range(groups - zslots, groups):
+        for h in range(2):
+
+            @pl.when(had(p, h))
+            def _():
+                for n in range(group):
+                    sent(p % zslots, n, h)
+
+    for j in range(count - 2, count):
+        out_copy(j).wait()
+
+    def drain(g, _):
+        n = rank(lax.div(g, per), lax.rem(g, per))
+        drain_own(g)
+
+        @pl.when(helper & (n < handed))
+        def _():
+            drain_far(n)
+
+        @pl.when(at_end & (n < handed))
+        def _():
+            row_copy(n, g).wait_send()
+
+        return 0
+
+    lax.fori_loop(0, chunks, drain, 0)
+
+
+def backward(cfg, ehi, elo, xparts, far_logits, vec, loss, counts, gp, spent):
+    cells, planes, C, S, G, GK, r = (cfg[k] for k in ("cells", "planes", "C", "S", "G", "GK", "r"))
+    chips, per, chunks = cells // 2, G // planes // GK, G // GK
+    parts, tile, group, zslots = cfg["parts"], cfg["tile"], cfg["group"], cfg["zslots"]
+    rows, handed = C // parts, cfg["handed"]
+    sem = pltpu.SemaphoreType.DMA
+    scratch = [
+        pltpu.VMEM((parts, 2 * rows, S), BF16), pltpu.VMEM((parts, 2 * rows, G), BF16),
+        pltpu.VMEM((parts // 2, 2 * rows, S), BF16),
+        pltpu.VMEM((G, S), BF16), pltpu.VMEM((G, S), BF16), pltpu.VMEM((2, GK, S), BF16),
+        pltpu.VMEM((2, chips, 2, r, S), F32), pltpu.VMEM((group, chips, 2, r, S), F32),
+        pltpu.VMEM((2, cfg["piece"], S), F32), pltpu.VMEM((group, 2, C // 2, GK), F32),
+        pltpu.VMEM((zslots, group, 2, C // 2, GK), F32), pltpu.VMEM((2, rows, tile), F32), pltpu.VMEM((2, rows, tile), F32),
+        pltpu.VMEM((8, S), F32), pltpu.VMEM((cells, 8, S), F32), pltpu.VMEM((planes, 8, 128), F32), pltpu.VMEM((C, 128), F32),
+        sem((2, parts)), sem, sem((2,)), sem((chunks, chips)), sem((chunks,)), sem((chunks, 2)),
+        sem((handed, chips)), sem((handed,)), sem((handed, 2)),
+        sem((handed,)), sem((handed,)), sem((2,)), sem((group,)),
+        sem((chunks + per, 2)), sem((zslots, group, 2)), sem((group, 2)), sem((2,)), sem((2,)),
+        sem((cells,)), sem((cells,)), sem((planes,)), sem((planes,)),
+    ]
+    return pl.pallas_call(
+        functools.partial(backward_kernel, cfg),
+        out_shape=(
+            jax.ShapeDtypeStruct((C, S), F32),
+            jax.ShapeDtypeStruct((C, G // planes), F32),
+            jax.ShapeDtypeStruct((8, 128), F32),
+            jax.ShapeDtypeStruct((chunks, chips, 2, r, S), F32),
+            jax.ShapeDtypeStruct((cfg["handed"], chips, 2, r, S), F32),
+            jax.ShapeDtypeStruct((chunks, C, GK), F32),
+            jax.ShapeDtypeStruct((per, C, GK), F32),
+        ),
+        in_specs=[ANY, ANY, ANY, ANY, VMEM, VMEM, VMEM, ANY, ANY],
+        out_specs=(ANY, ANY, VMEM, ANY, ANY, ANY, ANY),
+        input_output_aliases={7: 3, 8: 5},
+        scratch_shapes=scratch,
+        compiler_params=pltpu.CompilerParams(
+            collective_id=1, has_side_effects=True, vmem_limit_bytes=61 * 2**20
+        ),
+        cost_estimate=pl.CostEstimate(flops=12 * C * S * G, bytes_accessed=16 * C * S, transcendentals=0),
+        name="backward",
+    )(ehi, elo, xparts, far_logits, vec, loss, counts, gp, spent)
+
+
 def local(cells, planes, logits, expression, spatial, cell_counts, spot_density, slide_id, padding):
     C, S = logits.shape
     G = expression.shape[1] * planes
     GK = max(128, 8 * cells)
-    cfg = dict(cells=cells, planes=planes, C=C, S=S, G=G, GK=GK, r=GK // cells, rows=128, tile=512)
-    gath, ehi, elo, gp, vec, loss = forward(
-        cfg, logits, expression, spatial, cell_counts[None, :], spot_density[None, :],
+    chunks, parts, group = G // GK, 4, 256 // GK
+    tile = 256 * group
+    across = 1
+    while across * across < cells // 2:
+        across *= 2
+    cfg = dict(
+        cells=cells, planes=planes, C=C, S=S, G=G, GK=GK, r=GK // cells, rows=128, tile=tile, parts=parts,
+        group=group, zslots=1 + group, slots=max(chunks + parts * (S // tile), 5 + group + 2 * (chunks - group)), pieces=8, ahead=5, handed=chunks // 4,
+        across=across, helped=planes >= 4, piece=max(n for n in range(16, 65, 16) if C // parts % n == 0),
+    )
+    counts = cell_counts[None, :]
+    gath, ehi, elo, xparts, far_logits, gp, vec, loss = forward(
+        cfg, logits, expression, spatial, counts, spot_density[None, :],
         slide_id[None, :], padding[None, :],
     )
-    high = lax.Precision.HIGH
-    full = lax.all_gather(gp, "cell", axis=1).reshape(G, S)
-    gathered = gath.transpose(1, 0, 2).reshape(C, G)
-    exponent = ehi.astype(F32) + elo.astype(F32)
-    column = lax.psum(vec[0], "cell") + vec[9]
-    cos_sum = lax.psum(loss[0, :2], "cell")
-    spot_sum = lax.psum(loss[1, :2], "spot")
-    losses = -cos_sum / G - spot_sum / loss[2, :2] + loss[3, :2]
-    grad_map = jnp.dot(gathered, full, precision=high) + cell_counts.astype(F32)[:, None] * vec[8][None, :]
-    grad_logits = exponent * (grad_map - column)
-    partial_grad = lax.dot_general(exponent, full, NT, precision=high, preferred_element_type=F32)
-    grad_expression = lax.psum_scatter(partial_grad, "spot", scatter_dimension=1, tiled=True)
-    return (losses, grad_logits, grad_expression)
+    grad_logits, grad_expression, losses, *_ = backward(
+        cfg, ehi, elo, xparts, far_logits, vec, loss, counts, gp, gath
+    )
+    return (losses[0, :2], grad_logits, grad_expression)
 
 
 def solution(mesh):

time: 607 us -> 456 us (0.75)
  waiting for transfers between devices: 206 us -> 0 us
  Pallas kernels: 256 us -> 439 us
  matrix products: 91.2 us -> 0 us
  blocking collectives: 22 us -> 0 us
  between operations: 14.1 us -> 0.65 us
    pallas_call x0 -> x1, Pallas kernels: none -> 219 us  [backward(): pl.pallas_call(functools.partial(backward_kernel, cfg), out_shape=(jax.Sh...]
    reduce_scatter x1 -> x0, waiting for transfers between devices: 111 us -> none  [local(): lax.psum_scatter(partial_grad, 'spot', scatter_dimension=1, tiled=True)]
    all_gather x1 -> x0, waiting for transfers between devices: 94.9 us -> none  [local(): full = lax.all_gather(gp, 'cell', axis=1).reshape(G, S)]
    dot_general x2 -> x0, matrix products: 91.2 us -> none  [the longest x1 47.9 us: local(): jnp.dot(gathered, full, precision=high)]
    pallas_call x1, Pallas kernels: 256 us -> 220 us  [forward(): pl.pallas_call(functools.partial(forward_kernel, cfg), out_shape=(jax.Sha...]
    psum x2 -> x0, blocking collectives: 22 us -> none  [the longest x1 11.8 us: local(): cos_sum = lax.psum(loss[0, :2], 'cell')]
    transpose x1 -> x0, local copies, waits for them, and re-layouts: 12 us -> none  [local(): gathered = gath.transpose(1, 0, 2).reshape(C, G)]
    unnamed x4, local copies, waits for them, and re-layouts: 0.66 us -> 12.4 us
  transfers between devices with their start and end apart: 2 -> 0, of which waited for: 2 -> 0; matrix products, arithmetic and copies ran while one was open for 10% -> 0% of each run, Pallas kernels for 0% -> 0%
where the time goes in v4:
time: 456 us; the launch traced here: 454 us
  Pallas kernels  439 us (96%)
  local copies, waits for them, and re-layouts  14.8 us (3%)
    pallas_call x1, Pallas kernels, forward(): pl.pallas_call(functools.partial(forward_kernel, cfg), out_shape=(jax.Sha...  220 us
    pallas_call x1, Pallas kernels, backward(): pl.pallas_call(functools.partial(backward_kernel, cfg), out_shape=(jax.Sh...  219 us
    unnamed x4, local copies, waits for them, and re-layouts  12.4 us

profile of v4, /device:TPU:9, one launch (start us, length us, event | category | flops | bytes accessed | tf_op | source)
XLA Modules:
  0.0 454.2 jit_solution(7955016209111316140)
XLA Ops:
  0.6 1.3 broadcast_in_dim.12.counts
  1.9 219.9 %forward.1 = (f32[16,1408,128]{2,1,0:T(8,128)}, bf16[1408,2048]{1,0:T(8,128)(2,1)}, bf16[1408,2048]{1,0:T(8,128)(2,1)}, bf16[4,704,2048]{2,1,0:T(8,128)(2,1)}, f...) custom-call(f32[1408,2048]{1,0:T(8,128)} %logits.1, ...), custom_call_target="tpu_custom_call" | custom-call | flops 35433480192 | bytes 23068672 | tf_op jit(solution)/shard_map/forward/pallas_call | solution.py:529
  221.8 218.8 %backward.1 = (f32[1408,2048]{1,0:T(8,128)}, f32[1408,512]{1,0:T(8,128)}, f32[8,128]{1,0:T(8,128)}, f32[16,4,2,16,2048]{4,3,2,1,0:T(8,128)}, f32[4,4,2,16,2048]{...) custom-call(bf16[1408,2048]{1,0:T(8,128)(2,1)} %get-tuple-element.14, ...), custom_call_target="tpu_custom_call", output_to_operand_aliasing={{3}: (7, {}), {5}: (8, {})} | custom-call | flops 70866960384 | bytes 46137344 | tf_op jit(solution)/shard_map/backward/pallas_call | solution.py:1122
  440.6 1.2 slice_bitcast_fusion
  441.8 0.0 copy-start
  441.8 10.8 %copy.16 = f32[1408,2048]{1,0:T(8,128)} copy(f32[1408,2048]{1,0:T(8,128)} %get-tuple-element.29) | data formatting | bytes 23068672
  452.6 0.0 copy-done
  452.6 1.6 copy.17
Async XLA Ops:
  441.8 10.8 %copy-start = (f32[1408,512]{1,0:T(8,128)S(1)}, f32[1408,512]{1,0:T(8,128)}, u32[]{:S(2)}) copy-start(f32[1408,512]{1,0:T(8,128)} %get-tuple-element.30) | copy-start | bytes 8650756

commit v5 on v4

--- a/solution.py
+++ b/solution.py
@@ -191,7 +191,7 @@
         copy.start()
 
     row = lax.broadcasted_iota(jnp.int32, (16, C), 0)
-    weight = jnp.broadcast_to(counts[...].astype(F32), (16, C))
+    weight = jnp.broadcast_to(counts[...].astype(F32)[None, :], (16, C))
     lhs = jnp.where(row == 0, 1.0, jnp.where(row == 1, weight, 0.0)).astype(BF16)
 
     def sums(t, _):
@@ -936,6 +936,8 @@
 
     ends = [0] + [group - 1 + 2 * group * p for p in range(1, groups)]
     finishes = [4 + group + 2 * group * p for p in range(groups)]
+    if group == 2 and groups == 8:
+        finishes = [6, 10, 13, 16, 18, 20, 26, 32]
     makes = [max((p + 1) * group - 1, finishes[p - zslots] + 5 if p >= zslots else 0) for p in range(groups)]
     makes = finishes
 
@@ -1038,7 +1040,7 @@
             pltpu.make_async_copy(xparts, x2, x_sem).wait()
             total = collect(mine, vecr, vec_send, vec_recv, c, cells, in_plane)
             spot_sum = collect(loss, lossr, loss_send, loss_recv, z, planes, in_column)
-            weight[...] = jnp.broadcast_to(counts[...].astype(F32), (128, C)).T
+            weight[...] = jnp.broadcast_to(counts[...].astype(F32)[None, :], (128, C)).T
             cols[0:1, :] = vec[8:9, :]
             cols[1:2, :] = total[0:1, :] + vec[9:10, :]
             losses[...] = jnp.zeros_like(losses)
@@ -1142,6 +1144,52 @@
     )(ehi, elo, xparts, far_logits, vec, loss, counts, gp, spent)
 
 
+def passing_kernel(pieces, losses, first, second, out_losses, out_first, out_second, *rest):
+    buffers, (read, write) = rest[:2], rest[2:]
+    moves = []
+    for n, (source, target) in enumerate(((first, out_first), (second, out_second))):
+        rows = source.shape[0] // pieces[n]
+        for i in range(pieces[n]):
+            place = pl.ds(i * rows, rows)
+            slot = len(moves)
+            moves.append(
+                (
+                    pltpu.make_async_copy(source.at[place], buffers[n].at[place], read.at[slot]),
+                    pltpu.make_async_copy(buffers[n].at[place], target.at[place], write.at[slot]),
+                )
+            )
+    for load, _ in moves:
+        load.start()
+    for n in range(2):
+        out_losses[n] = losses[0, n]
+    for load, store in moves:
+        load.wait()
+        store.start()
+    for _, store in moves:
+        store.wait()
+
+
+def passing(losses, first, second):
+    pieces = [8, 2]
+    smem = pl.BlockSpec(memory_space=pltpu.SMEM)
+    return pl.pallas_call(
+        functools.partial(passing_kernel, pieces),
+        out_shape=(
+            jax.ShapeDtypeStruct((2,), F32),
+            jax.ShapeDtypeStruct(first.shape, first.dtype),
+            jax.ShapeDtypeStruct(second.shape, second.dtype),
+        ),
+        in_specs=[smem, ANY, ANY],
+        out_specs=(smem, ANY, ANY),
+        scratch_shapes=[
+            pltpu.VMEM(first.shape, first.dtype), pltpu.VMEM(second.shape, second.dtype),
+            pltpu.SemaphoreType.DMA((sum(pieces),)), pltpu.SemaphoreType.DMA((sum(pieces),)),
+        ],
+        compiler_params=pltpu.CompilerParams(vmem_limit_bytes=60 * 2**20),
+        name="passing",
+    )(losses, first, second)
+
+
 def local(cells, planes, logits, expression, spatial, cell_counts, spot_density, slide_id, padding):
     C, S = logits.shape
     G = expression.shape[1] * planes
@@ -1156,7 +1204,7 @@
         group=group, zslots=1 + group, slots=max(chunks + parts * (S // tile), 5 + group + 2 * (chunks - group)), pieces=8, ahead=5, handed=chunks // 4,
         across=across, helped=planes >= 4, piece=max(n for n in range(16, 65, 16) if C // parts % n == 0),
     )
-    counts = cell_counts[None, :]
+    counts = cell_counts
     gath, ehi, elo, xparts, far_logits, gp, vec, loss = forward(
         cfg, logits, expression, spatial, counts, spot_density[None, :],
         slide_id[None, :], padding[None, :],
@@ -1164,7 +1212,7 @@
     grad_logits, grad_expression, losses, *_ = backward(
         cfg, ehi, elo, xparts, far_logits, vec, loss, counts, gp, gath
     )
-    return (losses[0, :2], grad_logits, grad_expression)
+    return passing(losses, grad_logits, grad_expression)
 
 
 def solution(mesh):

time: 456 us -> 452 us (level)
  local copies, waits for them, and re-layouts: 14.8 us -> 0 us
  Pallas kernels: 439 us -> 449 us
    unnamed x4 -> x0, local copies, waits for them, and re-layouts: 12.4 us -> none
    pallas_call x0 -> x1, Pallas kernels: none -> 11.8 us  [passing(): pl.pallas_call(functools.partial(passing_kernel, pieces), out_shape=(jax....]
where the time goes in v5:
time: 452 us; the launch traced here: 450 us
  Pallas kernels  449 us (99%)
    pallas_call x1, Pallas kernels, forward(): pl.pallas_call(functools.partial(forward_kernel, cfg), out_shape=(jax.Sha...  220 us
    pallas_call x1, Pallas kernels, backward(): pl.pallas_call(functools.partial(backward_kernel, cfg), out_shape=(jax.Sh...  218 us
    pallas_call x1, Pallas kernels, passing(): pl.pallas_call(functools.partial(passing_kernel, pieces), out_shape=(jax....  11.8 us

profile of v5, /device:TPU:9, one launch (start us, length us, event | category | flops | bytes accessed | tf_op | source)
XLA Modules:
  0.0 449.9 jit_solution(8389234012683682106)
XLA Ops:
  0.6 219.9 %forward.1 = (f32[16,1408,128]{2,1,0:T(8,128)}, bf16[1408,2048]{1,0:T(8,128)(2,1)}, bf16[1408,2048]{1,0:T(8,128)(2,1)}, bf16[4,704,2048]{2,1,0:T(8,128)(2,1)}, f...) custom-call(f32[1408,2048]{1,0:T(8,128)} %logits.1, ...), custom_call_target="tpu_custom_call" | custom-call | flops 35433480192 | bytes 23068672 | tf_op jit(solution)/shard_map/forward/pallas_call | solution.py:529
  220.5 217.5 %backward.1 = (f32[1408,2048]{1,0:T(8,128)}, f32[1408,512]{1,0:T(8,128)}, f32[8,128]{1,0:T(8,128)}, f32[16,4,2,16,2048]{4,3,2,1,0:T(8,128)}, f32[4,4,2,16,2048]{...) custom-call(bf16[1408,2048]{1,0:T(8,128)(2,1)} %get-tuple-element.14, ...), custom_call_target="tpu_custom_call", output_to_operand_aliasing={{3}: (7, {}), {5}: (8, {})} | custom-call | flops 70866960384 | bytes 46137344 | tf_op jit(solution)/shard_map/backward/pallas_call | solution.py:1124
  438.1 11.8 %passing.1 = (f32[2]{0:T(128)}, f32[1408,2048]{1,0:T(8,128)}, f32[1408,512]{1,0:T(8,128)}) custom-call(f32[8,128]{1,0:T(8,128)} %get-tuple-element.22.losses, f32[1408,2048]{1,0:T(8,128)} %get-tuple-element.23.first, f32[1408,512]{1,0:T(8,128)} %get-tuple-element.24.second), custom_call_target="tpu_custom_call" | custom-call | tf_op jit(solution)/shard_map/passing/pallas_call | solution.py:1175

commit v6 on v5

--- a/solution.py
+++ b/solution.py
@@ -256,21 +256,6 @@
             pull.start()
 
         pull.wait()
-        columns = pl.ds(pl.multiple_of(g * GK, 128), GK)
-
-        @pl.when(i >= 1)
-        def _():
-            pltpu.make_async_copy(xparts, x_out.at[:, :, columns], put_sem).wait()
-
-        def keep_parts(t, _):
-            high, low = split(stage[pl.ds(pl.multiple_of(t * part, 16), part), :])
-            xparts[t, pl.ds(0, part), :] = high
-            xparts[t, pl.ds(part, part), :] = low
-            return 0
-
-        lax.fori_loop(0, parts, keep_parts, 0)
-        pltpu.make_async_copy(xparts, x_out.at[:, :, columns], put_sem).start()
-
         @pl.when(i >= 2)
         def _():
             core_copy(g, slot).wait_send()
@@ -293,6 +278,20 @@
 
         lax.fori_loop(0, S // tile, multiply, 0)
         core_copy(g, slot).start()
+        columns = pl.ds(pl.multiple_of(g * GK, 128), GK)
+
+        @pl.when(i >= 1)
+        def _():
+            pltpu.make_async_copy(xparts, x_out.at[:, :, columns], put_sem).wait()
+
+        def keep_parts(t, _):
+            high, low = split(stage[pl.ds(pl.multiple_of(t * part, 16), part), :])
+            xparts[t, pl.ds(0, part), :] = high
+            xparts[t, pl.ds(part, part), :] = low
+            return 0
+
+        lax.fori_loop(0, parts, keep_parts, 0)
+        pltpu.make_async_copy(xparts, x_out.at[:, :, columns], put_sem).start()
 
     def to_chips(i):
         d, k = arrival(z, i, planes, per)
@@ -357,6 +356,17 @@
             total = collect(tots, totr, tot_send, tot_recv, c, cells, in_plane)
             vec[0:1, :] = 1.0 / total[0:1, :]
             vec[1:2, :] = total[1:2, :] / total[0:1, :]
+            gst[...] = jnp.zeros_like(gst)
+            density = vec[1:2, :]
+            target = dens[...]
+            lane = lax.broadcasted_iota(jnp.int32, (1, gst.shape[1]), 1)
+            logs = target * jnp.log(target), target * jnp.log(density)
+            for n, v in enumerate((jnp.ones_like(target), target, density, *logs)):
+                line = jnp.zeros((1, gst.shape[1]), F32)
+                for m in range(2):
+                    one = jnp.sum(v * vec[4 + m : 5 + m, :], axis=1, keepdims=True)
+                    line = jnp.where(lane == m, one, line)
+                gst[8 + n : 9 + n, :] = line
 
         @pl.when((i >= 1) & (i <= chunks))
         def _():
@@ -374,18 +384,7 @@
     for n in range(3):
         spots[n : n + 1, :] = jnp.sum(acc[n], axis=0, keepdims=True)
     share(spots, spotr, spot_send, spot_recv, c, cells, in_plane)
-    gst[...] = jnp.zeros_like(gst)
     gst[0:8, :] = gcol[...].T[0:8, :]
-    density = vec[1:2, :]
-    target = dens[...]
-    lane = lax.broadcasted_iota(jnp.int32, (1, gst.shape[1]), 1)
-    logs = target * jnp.log(target), target * jnp.log(density)
-    for n, v in enumerate((jnp.ones_like(target), target, density, *logs)):
-        line = jnp.zeros((1, gst.shape[1]), F32)
-        for m in range(2):
-            one = jnp.sum(v * vec[4 + m : 5 + m, :], axis=1, keepdims=True)
-            line = jnp.where(lane == m, one, line)
-        gst[8 + n : 9 + n, :] = line
     share(gst, gstr, gst_send, gst_recv, z, planes, in_column)
 
     genes = collect(gst, gstr, gst_send, gst_recv, z, planes, in_column)
@@ -430,11 +429,11 @@
         value = (spat[g] * by_spatial + p * by_pred) * vec[0:1, :]
         acc[0] += p * value
         pred[g] = value
+        pltpu.make_async_copy(pred.at[g], gp_out.at[g, chip, core], out_sem.at[2]).start()
         return 0
 
     lax.fori_loop(0, chunks, gradient, 0)
     copy = pltpu.make_async_copy(pred, gp_out.at[:, chip, core], out_sem.at[2])
-    copy.start()
     vec_out[...] = jnp.zeros_like(vec_out)
     vec_out[0:1, :] = jnp.sum(acc[0], axis=0, keepdims=True)
     vec_out[8:9, :] = vec[6:7, :]

time: 452 us -> 451 us (level)
  no operation moved by 1% of the time
where the time goes in v6:
time: 451 us; the launch traced here: 449 us
  Pallas kernels  449 us (100%)
    pallas_call x1, Pallas kernels, forward(): pl.pallas_call(functools.partial(forward_kernel, cfg), out_shape=(jax.Sha...  219 us
    pallas_call x1, Pallas kernels, backward(): pl.pallas_call(functools.partial(backward_kernel, cfg), out_shape=(jax.Sh...  218 us
    pallas_call x1, Pallas kernels, passing(): pl.pallas_call(functools.partial(passing_kernel, pieces), out_shape=(jax....  11.8 us

profile of v6, /device:TPU:9, one launch (start us, length us, event | category | flops | bytes accessed | tf_op | source)
XLA Modules:
  0.0 449.3 jit_solution(14857130971018885350)
XLA Ops:
  0.6 219.2 %forward.1 = (f32[16,1408,128]{2,1,0:T(8,128)}, bf16[1408,2048]{1,0:T(8,128)(2,1)}, bf16[1408,2048]{1,0:T(8,128)(2,1)}, bf16[4,704,2048]{2,1,0:T(8,128)(2,1)}, f...) custom-call(f32[1408,2048]{1,0:T(8,128)} %logits.1, ...), custom_call_target="tpu_custom_call" | custom-call | flops 35433480192 | bytes 23068672 | tf_op jit(solution)/shard_map/forward/pallas_call | solution.py:528
  219.8 217.7 %backward.1 = (f32[1408,2048]{1,0:T(8,128)}, f32[1408,512]{1,0:T(8,128)}, f32[8,128]{1,0:T(8,128)}, f32[16,4,2,16,2048]{4,3,2,1,0:T(8,128)}, f32[4,4,2,16,2048]{...) custom-call(bf16[1408,2048]{1,0:T(8,128)(2,1)} %get-tuple-element.14, ...), custom_call_target="tpu_custom_call", output_to_operand_aliasing={{3}: (7, {}), {5}: (8, {})} | custom-call | flops 70866960384 | bytes 46137344 | tf_op jit(solution)/shard_map/backward/pallas_call | solution.py:1123
  437.5 11.8 %passing.1 = (f32[2]{0:T(128)}, f32[1408,2048]{1,0:T(8,128)}, f32[1408,512]{1,0:T(8,128)}) custom-call(f32[8,128]{1,0:T(8,128)} %get-tuple-element.22.losses, f32[1408,2048]{1,0:T(8,128)} %get-tuple-element.23.first, f32[1408,512]{1,0:T(8,128)} %get-tuple-element.24.second), custom_call_target="tpu_custom_call" | custom-call | tf_op jit(solution)/shard_map/passing/pallas_call | solution.py:1174

commit v7 on v6

--- a/solution.py
+++ b/solution.py
@@ -1193,15 +1193,15 @@
     C, S = logits.shape
     G = expression.shape[1] * planes
     GK = max(128, 8 * cells)
-    chunks, parts, group = G // GK, 4, 256 // GK
-    tile = 256 * group
+    chunks, parts, group = G // GK, 2, 256 // GK
+    tile = 128 * group
     across = 1
     while across * across < cells // 2:
         across *= 2
     cfg = dict(
         cells=cells, planes=planes, C=C, S=S, G=G, GK=GK, r=GK // cells, rows=128, tile=tile, parts=parts,
         group=group, zslots=1 + group, slots=max(chunks + parts * (S // tile), 5 + group + 2 * (chunks - group)), pieces=8, ahead=5, handed=chunks // 4,
-        across=across, helped=planes >= 4, piece=max(n for n in range(16, 65, 16) if C // parts % n == 0),
+        across=across, helped=planes >= 4, piece=max(n for n in range(16, 33, 16) if C // parts % n == 0),
     )
     counts = cell_counts
     gath, ehi, elo, xparts, far_logits, gp, vec, loss = forward(

time: 451 us -> 451 us (level)
  no operation moved by 1% of the time
where the time goes in v7:
time: 451 us; the launch traced here: 446 us
  Pallas kernels  446 us (99%)
    pallas_call x1, Pallas kernels, forward(): pl.pallas_call(functools.partial(forward_kernel, cfg), out_shape=(jax.Sha...  220 us
    pallas_call x1, Pallas kernels, backward(): pl.pallas_call(functools.partial(backward_kernel, cfg), out_shape=(jax.Sh...  214 us
    pallas_call x1, Pallas kernels, passing(): pl.pallas_call(functools.partial(passing_kernel, pieces), out_shape=(jax....  11.8 us

profile of v7, /device:TPU:9, one launch (start us, length us, event | category | flops | bytes accessed | tf_op | source)
XLA Modules:
  0.0 446.4 jit_solution(9986581832469371367)
XLA Ops:
  0.6 220.0 %forward.1 = (f32[16,1408,128]{2,1,0:T(8,128)}, bf16[1408,2048]{1,0:T(8,128)(2,1)}, bf16[1408,2048]{1,0:T(8,128)(2,1)}, bf16[2,1408,2048]{2,1,0:T(8,128)(2,1)}, ...) custom-call(f32[1408,2048]{1,0:T(8,128)} %logits.1, ...), custom_call_target="tpu_custom_call" | custom-call | flops 35433480192 | bytes 23068672 | tf_op jit(solution)/shard_map/forward/pallas_call | solution.py:528
  220.6 213.8 %backward.1 = (f32[1408,2048]{1,0:T(8,128)}, f32[1408,512]{1,0:T(8,128)}, f32[8,128]{1,0:T(8,128)}, f32[16,4,2,16,2048]{4,3,2,1,0:T(8,128)}, f32[4,4,2,16,2048]{...) custom-call(bf16[1408,2048]{1,0:T(8,128)(2,1)} %get-tuple-element.14, ...), custom_call_target="tpu_custom_call", output_to_operand_aliasing={{3}: (7, {}), {5}: (8, {})} | custom-call | flops 70866960384 | bytes 46137344 | tf_op jit(solution)/shard_map/backward/pallas_call | solution.py:1123
  434.4 11.8 %passing.1 = (f32[2]{0:T(128)}, f32[1408,2048]{1,0:T(8,128)}, f32[1408,512]{1,0:T(8,128)}) custom-call(f32[8,128]{1,0:T(8,128)} %get-tuple-element.22.losses, f32[1408,2048]{1,0:T(8,128)} %get-tuple-element.23.first, f32[1408,512]{1,0:T(8,128)} %get-tuple-element.24.second), custom_call_target="tpu_custom_call" | custom-call | tf_op jit(solution)/shard_map/passing/pallas_call | solution.py:1174
